TPU v7x, 32 devices: a whole 2x2x4 slice. The times are simulated.
32 devices in a mesh: ctx: 8 (over y, x, core), head: 4 (over z).
Axes of the slice: x: 2, y: 2, z: 4, core: 2. Of those that a mesh axis runs over, the one named last changes fastest.
Arguments:
- queries: bfloat16 [1024, 64, 576], P('ctx', 'head'), may hold values from -64 to 64
- latents: bfloat16 [1024, 576], P('ctx'), may hold values from -6 to 6
- grad_out: bfloat16 [1024, 64, 512], P('ctx', 'head'), may hold values from -6 to 6
- block_order: int32 [8], replicated, may hold values from 0 to 7, each once
- doc_ids: int32 [1024], replicated, may hold values from 0 to 3, never falling along the last dimension, each value on 1 to 512 neighbouring positions
Outputs:
- out_lat: bfloat16 [1024, 64, 512], P('ctx', 'head')
- grad_queries: bfloat16 [1024, 64, 576], P('ctx', 'head')
- grad_latents: float32 [1024, 576], P('ctx')
Inputs may be any that keep to these rules, and one draw needn't show every extreme that they name: Each number appears once; shard i of the token dimension holds the 64 positions of block block_order[i] followed by those of block 15 - block_order[i]. `doc_ids`: never falling along positions; every document holds 1 to 512 positions and one holds exactly 512.
All inputs are finite; a program needn't handle non-finite values.
Results may differ from a plain program's by a relative error of at most 0.014.
Values may be sent and summed in bfloat16 or wider, within the bound.
A program may use at most 128 MiB of HBM per device.

v0:
```python
import math

import jax
import jax.numpy as jnp
from jax import lax
from jax.sharding import PartitionSpec as P

score_scale = 192.0 ** (-0.5)
far_below = -1e30


def token_layout(block_order, doc_ids, ctx_count, tok_dev):
    row_ids = jnp.arange(ctx_count * tok_dev, dtype=jnp.int32)
    half_len = tok_dev // 2
    owner_dev = row_ids // tok_dev
    within = row_ids % tok_dev
    low_block = jnp.take(block_order, owner_dev)
    block_ids = jnp.where(within < half_len, low_block, 2 * ctx_count - 1 - low_block)
    positions = block_ids * half_len + within % half_len
    return (positions, jnp.take(doc_ids, positions))


def over_blocks(running, key_rows, update):
    total_rows = key_rows.shape[0]
    block_rows = math.gcd(total_rows, 512)
    steps_count = total_rows // block_rows

    def one_block(block_index, state_now):
        key_block = lax.dynamic_slice_in_dim(key_rows, block_index * block_rows, block_rows, 0)
        return update(state_now, key_block, block_index * block_rows)

    return lax.fori_loop(0, steps_count, one_block, running)


def body(queries, latents, grad_out, block_order, doc_ids):
    tok_dev = queries.shape[0]
    heads_dev = queries.shape[1]
    full_width = queries.shape[2]
    lat_width = grad_out.shape[2]
    ctx_count = lax.axis_size("ctx")
    my_index = lax.axis_index("ctx")
    all_pos, all_doc = token_layout(block_order, doc_ids, ctx_count, tok_dev)
    my_pos = lax.dynamic_slice_in_dim(all_pos, my_index * tok_dev, tok_dev)
    my_doc = lax.dynamic_slice_in_dim(all_doc, my_index * tok_dev, tok_dev)

    def visibility(first_row, count_rows):
        key_pos = lax.dynamic_slice_in_dim(all_pos, first_row, count_rows)
        key_doc = lax.dynamic_slice_in_dim(all_doc, first_row, count_rows)
        allowed = (key_pos[None, :] <= my_pos[:, None]) & (key_doc[None, :] == my_doc[:, None])
        return allowed[:, None, :]

    def guarded(update):

        def wrapped(running, key_block, first_row):
            visible = visibility(first_row, key_block.shape[0])
            return update(running, key_block, visible)

        return wrapped

    def forward_update(running, key_block, visible):
        row_max, row_sum, weighted = running
        scores = (
            jnp.einsum("thw,kw->thk", queries, key_block, preferred_element_type=jnp.float32)
            * score_scale
        )
        scores = jnp.where(visible, scores, far_below)
        new_max = jnp.maximum(row_max, jnp.max(scores, axis=2, keepdims=True))
        expo_terms = jnp.where(visible, jnp.exp(scores - new_max), 0.0)
        factor = jnp.exp(row_max - new_max)
        row_sum = row_sum * factor + jnp.sum(expo_terms, axis=2, keepdims=True)
        weighted = weighted * factor + jnp.einsum(
            "thk,kc->thc",
            expo_terms.astype(jnp.bfloat16),
            key_block[:, :lat_width],
            preferred_element_type=jnp.float32,
        )
        return (new_max, row_sum, weighted)

    forward_block = guarded(forward_update)
    start_state = (
        jnp.full((tok_dev, heads_dev, 1), far_below, jnp.float32),
        jnp.zeros((tok_dev, heads_dev, 1), jnp.float32),
        jnp.zeros((tok_dev, heads_dev, lat_width), jnp.float32),
    )
    running = over_blocks(
        start_state, lax.all_gather(latents, "ctx", axis=0, tiled=True), forward_block
    )
    row_max, row_sum, weighted = running
    out_lat = (weighted / row_sum).astype(jnp.bfloat16)
    log_sum = row_max + jnp.log(row_sum)
    row_delta = jnp.sum(
        grad_out.astype(jnp.float32) * out_lat.astype(jnp.float32), axis=2, keepdims=True
    )

    def backward_with_start(running, key_block, first_row):
        visible = visibility(first_row, key_block.shape[0])
        grad_query, grad_lat = running
        count_rows = key_block.shape[0]
        scores = (
            jnp.einsum("thw,kw->thk", queries, key_block, preferred_element_type=jnp.float32)
            * score_scale
        )
        row_probs = jnp.where(visible, jnp.exp(jnp.where(visible, scores, log_sum) - log_sum), 0.0)
        grad_probs = jnp.einsum(
            "thc,kc->thk", grad_out, key_block[:, :lat_width], preferred_element_type=jnp.float32
        )
        grad_scores = (row_probs * (grad_probs - row_delta) * score_scale).astype(jnp.bfloat16)
        grad_query = grad_query + jnp.einsum(
            "thk,kw->thw", grad_scores, key_block, preferred_element_type=jnp.float32
        )
        key_term = jnp.einsum(
            "thk,thw->kw", grad_scores, queries, preferred_element_type=jnp.float32
        )
        value_term = jnp.einsum(
            "thk,thc->kc",
            row_probs.astype(jnp.bfloat16),
            grad_out,
            preferred_element_type=jnp.float32,
        )
        key_term = key_term + jnp.pad(value_term, ((0, 0), (0, full_width - lat_width)))
        current = lax.dynamic_slice_in_dim(grad_lat, first_row, count_rows, 0)
        grad_lat = lax.dynamic_update_slice_in_dim(grad_lat, current + key_term, first_row, 0)
        return (grad_query, grad_lat)

    grad_start = (
        jnp.zeros((tok_dev, heads_dev, full_width), jnp.float32),
        jnp.zeros((ctx_count * tok_dev, full_width), jnp.float32),
    )
    grad_query, grad_lat = over_blocks(
        grad_start, lax.all_gather(latents, "ctx", axis=0, tiled=True), backward_with_start
    )
    own_rows = lax.psum_scatter(grad_lat, "ctx", scatter_dimension=0, tiled=True)
    grad_latents = lax.psum(own_rows, "head")
    return (out_lat, grad_query.astype(jnp.bfloat16), grad_latents)


def solution(mesh):
    return jax.shard_map(
        body,
        mesh=mesh,
        in_specs=(P("ctx", "head", None), P("ctx", None), P("ctx", "head", None), P(), P()),
        out_specs=(P("ctx", "head", None), P("ctx", "head", None), P("ctx", None)),
        check_vma=False,
    )
```

profile of v0, /device:TPU:0, one launch (start us, length us, event | category | flops | bytes accessed | tf_op | source)
XLA Modules:
  0.0 196.1 jit_solution(15782683875663543745)
XLA Ops:
  7.2 0.0 copy-start
  7.2 0.0 copy-start.2
  7.2 0.0 all-gather.2.cloned.1.call-start
  7.2 0.7 all-gather.2.cloned.1.call-update
  7.9 0.0 reduce-scatter.2.cloned.1.call-start
  8.0 1.6 fusion.64
  9.7 4.2 %compare_select_fusion.4 = s32[1024,1]{0,1:T(1,128)S(1)} fusion(s32[]{:T(128)} %bitcast.1, s32[]{:T(128)} %bitcast.2, s32[]{:T(128)} %bitcast.3, s32[]{:T(128)} %bitcast.4, s32[]{:T(128)} %bitcast.5, s32[]{:T(128)} %bitcast.7, s32[]{:T(128)} %bitcast.6), kind=kLoop, calls=%fused_computation.67 | loop fusion | flops 23552 | bytes 4124 | tf_op jit(solution)/shard_map/jit(_take)/gather | solution.py:17
  13.8 0.7 broadcast_select_fusion
  14.5 0.0 copy-done
  14.6 4.5 %gather_fusion = s32[1024]{0:T(1024)S(1)} fusion(s32[1024]{0:T(1024)S(1)} %copy-done, s32[1024]{0:T(1024)S(1)} %broadcast_clamp_fusion), kind=kCustom, calls=%fused_computation | custom fusion | bytes 12288 | tf_op jit(solution)/shard_map/jit(_take)/gather | solution.py:20
  19.1 0.1 dynamic_slice.67
  19.2 0.1 dynamic_slice.68
  19.3 0.0 copy-done.2
  19.3 3.1 %copy.37 = bf16[128,16,512]{0,2,1:T(8,128)(2,1)} copy(bf16[128,16,512]{2,1,0:T(8,128)(2,1)S(1)} %copy-done.2) | data formatting | bytes 4194304
  22.3 14.4 %all-gather.2.cloned.1.call-done = bf16[1024,576]{0,1:T(8,128)(2,1)} async-done(((bf16[128,576]{0,1:T(8,128)(2,1)}), bf16[1024,576]{0,1:T(8,128)(2,1)}) %all-gather.2.cloned.1.call-update) | async-done | bytes 1179664 | tf_op jit(solution)/shard_map/all_gather | solution.py:86
  36.8 28.7 %while.36 = (s32[]{:T(128)}, f32[128,16,1]{0,1,2:T(8,128)S(1)}, f32[128,16,1]{0,1,2:T(8,128)S(1)}, f32[128,16,512]{2,0,1:T(8,128)}, s32[1024]{0:T(1024)S(1)}, /*...) while((s32[]{:T(128)}, f32[128,16,1]{0,1,2:T(8,128)S(1)}, ...), condition=%wide.region_3.4_spmd.clone, body=%wide.region_0.3_spmd.clone.sunk | while | flops 2298687488 | bytes 41628904 | solution.py:32
  36.8 0.1 dynamic_slice.100
  36.9 0.1 dynamic_slice.101
  36.9 0.2 compare_and_fusion.4
  37.1 5.8 %fusion.93 = (f32[128,16]{0,1:T(8,128)S(1)}, f32[512,128,16]{1,0,2:T(8,128)}) fusion(pred[128,512]{0,1:T(8,128)(4,1)S(1)} %compare_and_fusion.4, bf16[128,16,576]{0,2,1:T(8,128)(2,1)} %get-tuple-element.813, bf16[1024,576]{0,1:T(8,128)(2,1)} %get-tuple-element.812, s32[]{:T(128)S(6)} %select_n.356), kind=kOutput, calls=%fused_computation.5.clone.1 | convolution fusion | flops 1211103232 | bytes 7217156 | tf_op jit(solution)/shard_map/while/body/eval_jaxpr/thw,kw->thk/dot_general | solution.py:63
  42.9 0.0 copy-start.1
  43.0 6.5 %fusion.96 = f32[128,16,512]{2,0,1:T(8,128)} fusion(f32[128,16,512]{2,0,1:T(8,128)} %get-tuple-element.793, f32[512,128,16]{1,0,2:T(8,128)} %get-tuple-element.762, f32[128,16]{0,1:T(8,128)S(1)} %get-tuple-element.763, f32[128,16]{0,1:T(8,128)S(1)} %bitcast.138, pred[]{:T(512)S(6)} %compare.84, pred[128,512]{0,1:T(8,128)(4,1)S(1)} %compare_and_fusion.4, ...), kind=kOutput, calls=%fused_computation.3.clone.1 | convolution fusion | flops 1082130432 | bytes 13189125 | tf_op jit(solution)/shard_map/while/body/eval_jaxpr/thk,kc->thc/dot_general | solution.py:71
  49.4 0.0 copy-done.1
  49.4 1.0 fusion.95
  50.5 0.1 dynamic_slice.100
  50.6 0.1 dynamic_slice.101
  50.6 0.2 compare_and_fusion.4
  50.9 5.8 %fusion.93 = (f32[128,16]{0,1:T(8,128)S(1)}, f32[512,128,16]{1,0,2:T(8,128)}) fusion(pred[128,512]{0,1:T(8,128)(4,1)S(1)} %compare_and_fusion.4, bf16[128,16,576]{0,2,1:T(8,128)(2,1)} %get-tuple-element.813, bf16[1024,576]{0,1:T(8,128)(2,1)} %get-tuple-element.812, s32[]{:T(128)S(6)} %select_n.356), kind=kOutput, calls=%fused_computation.5.clone.1 | convolution fusion | flops 1211103232 | bytes 7217156 | tf_op jit(solution)/shard_map/while/body/eval_jaxpr/thw,kw->thk/dot_general | solution.py:63
  56.7 0.0 copy-start.1
  56.7 7.8 %fusion.96 = f32[128,16,512]{2,0,1:T(8,128)} fusion(f32[128,16,512]{2,0,1:T(8,128)} %get-tuple-element.793, f32[512,128,16]{1,0,2:T(8,128)} %get-tuple-element.762, f32[128,16]{0,1:T(8,128)S(1)} %get-tuple-element.763, f32[128,16]{0,1:T(8,128)S(1)} %bitcast.138, pred[]{:T(512)S(6)} %compare.84, pred[128,512]{0,1:T(8,128)(4,1)S(1)} %compare_and_fusion.4, ...), kind=kOutput, calls=%fused_computation.3.clone.1 | convolution fusion | flops 1082130432 | bytes 13189125 | tf_op jit(solution)/shard_map/while/body/eval_jaxpr/thk,kc->thc/dot_general | solution.py:71
  64.5 0.0 copy-done.1
  64.5 1.0 fusion.95
  65.5 0.1 copy.35
  65.6 6.4 %multiply_reduce_fusion = (f32[128,16]{1,0:T(8,128)S(1)}, bf16[128,16,512]{2,1,0:T(8,128)(2,1)}) fusion(bf16[128,16,512]{2,1,0:T(8,128)(2,1)S(1)} %copy-done.2, f32[128,16]{1,0:T(8,128)S(1)} %copy.35, f32[128,16,512]{2,0,1:T(8,128)} %get-tuple-element.461), kind=kLoop, calls=%fused_computation.61 | loop fusion | flops 6289408 | bytes 8404992 | tf_op jit(solution)/shard_map/reduce_sum | solution.py:91
  72.1 1.7 broadcast_in_dim.177
  73.8 0.0 copy-done.3
  73.8 33.1 %while.37 = (s32[]{:T(128)}, f32[128,16,576]{0,2,1:T(8,128)}, f32[1024,576]{0,1:T(8,128)}, s32[1024]{0:T(1024)S(1)}, s32[128]{0:T(128)S(1)}, /*index=5*/s32[1024...) while((s32[]{:T(128)}, f32[128,16,576]{0,2,1:T(8,128)}, ...), condition=%wide.region_6.7_spmd.clone, body=%wide.region_5.6_spmd.clone.sunk | while | flops 5788139520 | bytes 61445404 | solution.py:32
  73.8 0.1 dynamic_slice.105
  73.9 0.1 dynamic_slice.106
  74.0 0.2 compare_and_fusion.5
  74.2 3.7 %fusion.106 = f32[512,128,16]{1,0,2:T(8,128)S(1)} fusion(bf16[128,16,576]{0,2,1:T(8,128)(2,1)} %get-tuple-element.858, bf16[1024,576]{0,1:T(8,128)(2,1)S(1)} %get-tuple-element.857, s32[]{:T(128)S(6)} %select_n.361), kind=kOutput, calls=%fused_computation.48.clone.1 | convolution fusion | flops 1207959552 | bytes 7143428 | tf_op jit(solution)/shard_map/while/body/eval_jaxpr/thw,kw->thk/dot_general | solution.py:100
  77.9 2.3 %fusion.107 = bf16[128,16,512]{0,2,1:T(8,128)(2,1)S(1)} fusion(f32[512,128,16]{1,0,2:T(8,128)S(1)} %fusion.106, bf16[128,16,512]{0,2,1:T(8,128)(2,1)S(1)} %copy-done.4, f32[128,16]{0,1:T(8,128)S(1)} %bitcast.147, f32[128,16]{0,1:T(8,128)S(1)} %bitcast.145, pred[128,512]{0,1:T(8,128)(4,1)S(1)} %compare_and_fusion.5, ...), kind=kOutput, calls=%fused_computation.31.clone.1 | convolution fusion | flops 1082130432 | bytes 8994820 | tf_op jit(solution)/shard_map/while/body/eval_jaxpr/thc,kc->thk/dot_general | solution.py:104
  80.2 0.0 copy-start.5
  80.3 1.4 fusion.108
  81.7 0.2 copy-done.5
  81.9 3.7 %fusion.109 = f32[1024,576]{0,1:T(8,128)} fusion(f32[1024,576]{0,1:T(8,128)} %get-tuple-element.836, s32[]{:T(128)S(6)} %select_n.361, bf16[128,16,512]{0,2,1:T(8,128)(2,1)S(1)} %fusion.107, bf16[128,16,576]{0,2,1:T(8,128)(2,1)S(1)} %copy-done.5, f32[512,512]{0,1:T(8,128)S(1)} %fusion.108), kind=kOutput, calls=%fused_computation.46.clone.1 | convolution fusion | flops 1208549376 | bytes 7864324 | tf_op jit(solution)/shard_map/while/body/eval_jaxpr/thk,thw->kw/dot_general | solution.py:111
  85.6 3.6 %select_add_fusion.2 = f32[128,16,576]{0,2,1:T(8,128)} fusion(f32[128,16,576]{0,2,1:T(8,128)} %get-tuple-element.835, pred[]{:T(512)S(6)} %compare.85, bf16[128,16,512]{0,2,1:T(8,128)(2,1)S(1)} %fusion.107, bf16[1024,576]{0,1:T(8,128)(2,1)S(1)} %get-tuple-element.857, s32[]{:T(128)S(6)} %select_n.361), kind=kOutput, calls=%fused_computation.28.clone.1 | convolution fusion | flops 1210318848 | bytes 12124165 | tf_op jit(solution)/shard_map/while/body/eval_jaxpr/thk,kw->thw/dot_general | solution.py:108
  89.2 0.1 dynamic_slice.105
  89.3 0.1 dynamic_slice.106
  89.4 0.2 compare_and_fusion.5
  89.6 3.7 %fusion.106 = f32[512,128,16]{1,0,2:T(8,128)S(1)} fusion(bf16[128,16,576]{0,2,1:T(8,128)(2,1)} %get-tuple-element.858, bf16[1024,576]{0,1:T(8,128)(2,1)S(1)} %get-tuple-element.857, s32[]{:T(128)S(6)} %select_n.361), kind=kOutput, calls=%fused_computation.48.clone.1 | convolution fusion | flops 1207959552 | bytes 7143428 | tf_op jit(solution)/shard_map/while/body/eval_jaxpr/thw,kw->thk/dot_general | solution.py:100
  93.3 2.3 %fusion.107 = bf16[128,16,512]{0,2,1:T(8,128)(2,1)S(1)} fusion(f32[512,128,16]{1,0,2:T(8,128)S(1)} %fusion.106, bf16[128,16,512]{0,2,1:T(8,128)(2,1)S(1)} %copy-done.4, f32[128,16]{0,1:T(8,128)S(1)} %bitcast.147, f32[128,16]{0,1:T(8,128)S(1)} %bitcast.145, pred[128,512]{0,1:T(8,128)(4,1)S(1)} %compare_and_fusion.5, ...), kind=kOutput, calls=%fused_computation.31.clone.1 | convolution fusion | flops 1082130432 | bytes 8994820 | tf_op jit(solution)/shard_map/while/body/eval_jaxpr/thc,kc->thk/dot_general | solution.py:104
  95.6 0.0 copy-start.5
  95.6 1.4 fusion.108
  97.1 0.2 copy-done.5
  97.3 3.7 %fusion.109 = f32[1024,576]{0,1:T(8,128)} fusion(f32[1024,576]{0,1:T(8,128)} %get-tuple-element.836, s32[]{:T(128)S(6)} %select_n.361, bf16[128,16,512]{0,2,1:T(8,128)(2,1)S(1)} %fusion.107, bf16[128,16,576]{0,2,1:T(8,128)(2,1)S(1)} %copy-done.5, f32[512,512]{0,1:T(8,128)S(1)} %fusion.108), kind=kOutput, calls=%fused_computation.46.clone.1 | convolution fusion | flops 1208549376 | bytes 7864324 | tf_op jit(solution)/shard_map/while/body/eval_jaxpr/thk,thw->kw/dot_general | solution.py:111
  101.0 5.9 %select_add_fusion.2 = f32[128,16,576]{0,2,1:T(8,128)} fusion(f32[128,16,576]{0,2,1:T(8,128)} %get-tuple-element.835, pred[]{:T(512)S(6)} %compare.85, bf16[128,16,512]{0,2,1:T(8,128)(2,1)S(1)} %fusion.107, bf16[1024,576]{0,1:T(8,128)(2,1)S(1)} %get-tuple-element.857, s32[]{:T(128)S(6)} %select_n.361), kind=kOutput, calls=%fused_computation.28.clone.1 | convolution fusion | flops 1210318848 | bytes 12124165 | tf_op jit(solution)/shard_map/while/body/eval_jaxpr/thk,kw->thw/dot_general | solution.py:108
  106.9 0.0 reduce-scatter.2.cloned.1.call-update
  107.0 0.0 all-reduce.3.cloned.1.call-start
  107.0 42.6 %reduce-scatter.2.cloned.1.call-done = f32[128,576]{0,1:T(8,128)} async-done(((f32[1024,576]{0,1:T(8,128)}), f32[128,576]{0,1:T(8,128)}) %reduce-scatter.2.cloned.1.call-update) | async-done | bytes 294928 | tf_op jit(solution)/shard_map/reduce_scatter | solution.py:132
  149.6 0.0 all-reduce.3.cloned.1.call-update
  149.6 4.1 %convert_element_type.50 = bf16[128,16,576]{0,2,1:T(8,128)(2,1)} convert(f32[128,16,576]{0,2,1:T(8,128)} %get-tuple-element.464) | non-fusion elementwise | flops 1179648 | bytes 7077888 | tf_op jit(solution)/shard_map/convert_element_type | solution.py:134
  153.8 34.1 %all-reduce.3.cloned.1.call-done = f32[128,576]{0,1:T(8,128)} async-done(((f32[128,576]{0,1:T(8,128)}), f32[128,576]{0,1:T(8,128)}) %all-reduce.3.cloned.1.call-update) | async-done | bytes 294928 | tf_op jit(solution)/shard_map/psum | solution.py:133
  187.9 1.7 copy.75
  (21 shorter events, 0.2 us)
Async XLA Ops:
  7.2 7.4 %copy-start = (s32[1024]{0:T(1024)S(1)}, s32[1024]{0:T(1024)}, u32[]{:S(2)}) copy-start(s32[1024]{0:T(1024)} %param.13) | copy-start | bytes 12292
  7.2 12.1 %copy-start.2 = (bf16[128,16,512]{2,1,0:T(8,128)(2,1)S(1)}, bf16[128,16,512]{2,1,0:T(8,128)(2,1)}, u32[]{:S(2)}) copy-start(bf16[128,16,512]{2,1,0:T(8,128)(2,1)} %param.11) | copy-start | bytes 6291460
  7.2 29.6 %all-gather.2.cloned.1.call-start = ((), (), s32[]{:S(2)}) async-start(), calls=%async_computation.1 | async-start | bytes 1327104 | tf_op jit(solution)/shard_map/all_gather | solution.py:86
  7.9 141.7 %reduce-scatter.2.cloned.1.call-start = ((), (), s32[]{:S(2)}) async-start(), calls=%async_computation.2 | async-start | bytes 2654208 | tf_op jit(solution)/shard_map/reduce_scatter | solution.py:132
  42.9 6.5 %copy-start.1 = (f32[512,128,16]{1,0,2:T(8,128)S(1)}, f32[512,128,16]{1,0,2:T(8,128)}, u32[]{:S(2)}) copy-start(f32[512,128,16]{1,0,2:T(8,128)} %get-tuple-element.762) | copy-start | bytes 12582916 | tf_op jit(solution)/shard_map/while
  56.7 7.8 %copy-start.1 = (f32[512,128,16]{1,0,2:T(8,128)S(1)}, f32[512,128,16]{1,0,2:T(8,128)}, u32[]{:S(2)}) copy-start(f32[512,128,16]{1,0,2:T(8,128)} %get-tuple-element.762) | copy-start | bytes 12582916 | tf_op jit(solution)/shard_map/while
  65.6 8.2 %copy-start.3 = (bf16[1024,576]{0,1:T(8,128)(2,1)S(1)}, bf16[1024,576]{0,1:T(8,128)(2,1)}, u32[]{:S(2)}) copy-start(bf16[1024,576]{0,1:T(8,128)(2,1)} %get-tuple-element.873) | copy-start | bytes 3538948
  74.2 3.7 %copy-start.4 = (bf16[128,16,512]{0,2,1:T(8,128)(2,1)S(1)}, bf16[128,16,512]{0,2,1:T(8,128)(2,1)}, u32[]{:S(2)}) copy-start(bf16[128,16,512]{0,2,1:T(8,128)(2,1)} %get-tuple-element.860) | copy-start | bytes 6291460 | tf_op jit(solution)/shard_map/while
  80.2 1.7 copy-start.5
  89.6 3.7 %copy-start.4 = (bf16[128,16,512]{0,2,1:T(8,128)(2,1)S(1)}, bf16[128,16,512]{0,2,1:T(8,128)(2,1)}, u32[]{:S(2)}) copy-start(bf16[128,16,512]{0,2,1:T(8,128)(2,1)} %get-tuple-element.860) | copy-start | bytes 6291460 | tf_op jit(solution)/shard_map/while
  95.6 1.7 copy-start.5
  107.0 80.9 %all-reduce.3.cloned.1.call-start = ((), (), s32[]{:S(2)}) async-start(), calls=%async_computation.3 | async-start | bytes 589824 | tf_op jit(solution)/shard_map/psum | solution.py:133
Sparse Core Ops, SparseCore 0:
  9.9 26.8 all-gather.1
  107.1 42.4 reduce-scatter.1
  152.1 35.7 all-reduce.2
where the time goes:
time: 197 us; the launch traced here: 196 us
  waiting for transfers between devices  91.9 us (47%)
  matrix products  57.7 us (29%)
  other arithmetic  18.3 us (9%)
  local copies, waits for them, and re-layouts  14 us (7%)
  between operations  13.9 us (7%)
    reduce_scatter x1, waiting for transfers between devices, body(): lax.psum_scatter(grad_lat, 'ctx', scatter_dimension=0, tiled=True)  42.6 us
    psum x1, waiting for transfers between devices, body(): grad_latents = lax.psum(own_rows, 'head')  34.1 us
    all_gather x1, waiting for transfers between devices, body(): lax.all_gather(latents, 'ctx', axis=0, tiled=True)  14.4 us
    dot_general x2, matrix products, forward_update(): jnp.einsum('thk,kc->thc', expo_terms.astype(jnp.bfloat16), key_block[:, :...  14.3 us
    dot_general x2, matrix products, forward_update(): jnp.einsum('thw,kw->thk', queries, key_block, preferred_element_type=jnp....  11.6 us
    dot_general x2, matrix products, backward_with_start(): jnp.einsum('thk,kw->thw', grad_scores, key_block, preferred_element_type=...  9.49 us
    dot_general x2, matrix products, backward_with_start(): jnp.einsum('thk,thw->kw', grad_scores, queries, preferred_element_type=jn...  7.43 us
    dot_general x2, matrix products, backward_with_start(): jnp.einsum('thw,kw->thk', queries, key_block, preferred_element_type=jnp....  7.38 us
  transfers between devices with their start and end apart: 3, of which 3 were waited for; matrix products, arithmetic and copies ran while one was open for 9% of the time, Pallas kernels for 0%

commit v1 on v0

v1 whole, which is shorter than its diff:
```python
import functools

import jax
import jax.numpy as jnp
from jax import lax
from jax.experimental import pallas as pl
from jax.experimental.pallas import tpu as pltpu
from jax.sharding import PartitionSpec as P

score_scale = 192.0 ** (-0.5)
far_below = -1e30
DOCS = 4
KEY_TILE = 256
ROWS = 512
NT = (((1,), (1,)), ((), ()))
NN = (((1,), (0,)), ((), ()))
TN = (((0,), (0,)), ((), ()))


def dot(a, b, dims):
    return lax.dot_general(a, b, dims, preferred_element_type=jnp.float32)


def attention_kernel(
    shape, order_ref, docs_ref, q_ref, g_ref, lat_ref, out_ref, gq_ref, gl_ref,
    keys, grad_keys, scores, acc, acc_q, bounds, sems,
):
    n_ctx, half, heads, chunk_tok, lat = shape
    seq = 2 * half * n_ctx
    c = pl.program_id(0)
    me = lax.axis_index("ctx")

    def block_of(slot):
        low = order_ref[slot // 2]
        return low if slot % 2 == 0 else 2 * n_ctx - 1 - low

    @pl.when(c == 0)
    def _():
        copies = []
        for slot in range(2 * n_ctx):
            first = pl.multiple_of(block_of(slot) * half, half)
            copy = pltpu.make_async_copy(
                lat_ref.at[pl.ds(slot * half, half)], keys.at[pl.ds(first, half)], sems.at[slot]
            )
            copy.start()
            copies.append(copy)
        keys[pl.ds(seq, KEY_TILE)] = jnp.zeros((KEY_TILE, keys.shape[1]), keys.dtype)
        grad_keys[...] = jnp.zeros_like(grad_keys)
        bounds[0] = 0
        for number in range(1, DOCS):
            at = jnp.int32(0)
            step = seq // 2
            while step >= 1:
                at = jnp.where(docs_ref[at + step - 1] < number, at + step, at)
                step //= 2
            bounds[number] = at
        for copy in copies:
            copy.wait()

    low = order_ref[me]
    first_tok = c * chunk_tok
    block = jnp.where(first_tok < half, low, 2 * n_ctx - 1 - low)
    pos0 = block * half + lax.rem(first_tok, half)
    doc_start = jnp.int32(0)
    for number in range(1, DOCS):
        doc_start = jnp.where(bounds[number] <= pos0, bounds[number], doc_start)
    start = (doc_start // 16) * 16
    tiles = (pos0 + chunk_tok - start + KEY_TILE - 1) // KEY_TILE

    rows = chunk_tok * heads
    row_pos = pos0 + lax.broadcasted_iota(jnp.int32, (rows, 1), 0) // heads
    row_doc = jnp.zeros_like(row_pos)
    for number in range(1, DOCS):
        row_doc = jnp.where(bounds[number] <= row_pos, bounds[number], row_doc)
    q = q_ref[...]
    g = g_ref[...]

    def tile_at(i):
        return pl.ds(pl.multiple_of(start + i * KEY_TILE, 16), KEY_TILE)

    def first_pass(i, row_max):
        s = dot(q, keys[tile_at(i), :], NT) * score_scale
        key_pos = start + i * KEY_TILE + lax.broadcasted_iota(jnp.int32, (1, KEY_TILE), 1)
        s = jnp.where((key_pos <= row_pos) & (key_pos >= row_doc), s, far_below)
        scores[i] = s
        return jnp.maximum(row_max, jnp.max(s, axis=1, keepdims=True))

    row_max = lax.fori_loop(0, tiles, first_pass, jnp.full((rows, 1), far_below, jnp.float32))
    acc[...] = jnp.zeros_like(acc)

    def second_pass(i, row_sum):
        e = jnp.exp(scores[i] - row_max)
        scores[i] = e
        acc[...] += dot(e.astype(jnp.bfloat16), keys[tile_at(i), :lat], NN)
        return row_sum + jnp.sum(e, axis=1, keepdims=True)

    row_sum = lax.fori_loop(0, tiles, second_pass, jnp.zeros((rows, 1), jnp.float32))
    inverse = 1.0 / row_sum
    out = (acc[...] * inverse).astype(jnp.bfloat16)
    out_ref[...] = out
    delta = jnp.sum(g.astype(jnp.float32) * out.astype(jnp.float32), axis=1, keepdims=True)
    acc_q[...] = jnp.zeros_like(acc_q)

    def third_pass(i, carry):
        at = tile_at(i)
        grad_probs = dot(g, keys[at, :lat], NT)
        probs = scores[i] * inverse
        ds = (probs * (grad_probs - delta) * score_scale).astype(jnp.bfloat16)
        acc_q[...] += dot(ds, keys[at, :], NN)
        grad_keys[at, :] += dot(ds, q, TN)
        grad_keys[at, :lat] += dot(probs.astype(jnp.bfloat16), g, TN)
        return carry

    lax.fori_loop(0, tiles, third_pass, 0)
    gq_ref[...] = acc_q[...].astype(jnp.bfloat16)

    @pl.when(c == pl.num_programs(0) - 1)
    def _():
        for slot in range(2 * n_ctx):
            first = pl.multiple_of(block_of(slot) * half, half)
            gl_ref[pl.ds(slot * half, half), :] = grad_keys[pl.ds(first, half), :].astype(
                gl_ref.dtype
            )


def attention(queries, grad_out, all_lat, block_order, doc_ids, n_ctx, sum_type):
    tok, heads, width = queries.shape
    lat = grad_out.shape[2]
    half = tok // 2
    seq = tok * n_ctx
    chunk_tok = min(half, max(1, ROWS // heads))
    rows = chunk_tok * heads
    tile_count = seq // KEY_TILE + 1
    block = lambda w: pl.BlockSpec((rows, w), lambda c, *_: (c, 0))
    out, gq, gl = pl.pallas_call(
        functools.partial(attention_kernel, (n_ctx, half, heads, chunk_tok, lat)),
        grid_spec=pltpu.PrefetchScalarGridSpec(
            num_scalar_prefetch=2,
            grid=(tok // chunk_tok,),
            in_specs=[block(width), block(lat), pl.BlockSpec(memory_space=pl.ANY)],
            out_specs=[
                block(lat),
                block(width),
                pl.BlockSpec((seq, width), lambda c, *_: (0, 0)),
            ],
            scratch_shapes=[
                pltpu.VMEM((seq + KEY_TILE, width), jnp.bfloat16),
                pltpu.VMEM((seq + KEY_TILE, width), jnp.float32),
                pltpu.VMEM((tile_count, rows, KEY_TILE), jnp.float32),
                pltpu.VMEM((rows, lat), jnp.float32),
                pltpu.VMEM((rows, width), jnp.float32),
                pltpu.SMEM((DOCS,), jnp.int32),
                pltpu.SemaphoreType.DMA((2 * n_ctx,)),
            ],
        ),
        out_shape=[
            jax.ShapeDtypeStruct((tok * heads, lat), jnp.bfloat16),
            jax.ShapeDtypeStruct((tok * heads, width), jnp.bfloat16),
            jax.ShapeDtypeStruct((seq, width), sum_type),
        ],
        compiler_params=pltpu.CompilerParams(vmem_limit_bytes=48 * 1024 * 1024),
        cost_estimate=pl.CostEstimate(
            flops=14 * tok * heads * seq * lat // 2, bytes_accessed=12 << 20, transcendentals=0
        ),
    )(
        block_order, doc_ids,
        queries.reshape(tok * heads, width), grad_out.reshape(tok * heads, lat), all_lat,
    )
    return out.reshape(tok, heads, lat), gq.reshape(tok, heads, width), gl


def body(queries, latents, grad_out, block_order, doc_ids):
    n_ctx = lax.axis_size("ctx")
    all_lat = lax.all_gather(latents, "ctx", axis=0, tiled=True)
    out, gq, gl = attention(queries, grad_out, all_lat, block_order, doc_ids, n_ctx, jnp.float32)
    own_rows = lax.psum_scatter(gl, "ctx", scatter_dimension=0, tiled=True)
    return out, gq, lax.psum(own_rows, "head")


def solution(mesh):
    return jax.shard_map(
        body,
        mesh=mesh,
        in_specs=(P("ctx", "head", None), P("ctx", None), P("ctx", "head", None), P(), P()),
        out_specs=(P("ctx", "head", None), P("ctx", "head", None), P("ctx", None)),
        check_vma=False,
    )
```

time: 197 us -> 152 us (0.77)
  matrix products: 57.7 us -> 0 us
  Pallas kernels: 0 us -> 20.6 us
  other arithmetic: 18.3 us -> 0 us
  waiting for transfers between devices: 91.9 us -> 103 us
    dot_general x14 -> x0, matrix products: 57.7 us -> none  [the longest x2 14.3 us: forward_update(): jnp.einsum('thk,kc->thc', expo_terms.astype(jnp.bfloat16), key_block[:, :...]
    pallas_call x0 -> x1, Pallas kernels: none -> 20.6 us  [attention(): pl.pallas_call(functools.partial(attention_kernel, (n_ctx, half, heads, c...]
    unnamed x9 -> x12, local copies, waits for them, and re-layouts: 4.83 us -> 14.5 us
    all_gather x1, waiting for transfers between devices: 14.4 us -> 23.9 us  [body(): all_lat = lax.all_gather(latents, 'ctx', axis=0, tiled=True)]
    reduce_sum x3 -> x0, other arithmetic: 8.41 us -> none  [the longest x1 6.41 us: body(): jnp.sum(grad_out.astype(jnp.float32) * out_lat.astype(jnp.float32), axis=...]
    gather x2 -> x0, local copies, waits for them, and re-layouts: 6.14 us -> none  [the longest x1 4.53 us: token_layout(): return (positions, jnp.take(doc_ids, positions))]
    gather x4 -> x0, other arithmetic: 4.86 us -> none  [the longest x3 4.86 us: token_layout(): low_block = jnp.take(block_order, owner_dev)]
    convert_element_type x1 -> x0, other arithmetic: 4.15 us -> none  [body(): return (out_lat, grad_query.astype(jnp.bfloat16), grad_latents)]
  transfers between devices with their start and end apart: 3 -> 3, of which waited for: 3 -> 3; matrix products, arithmetic and copies ran while one was open for 9% -> 5% of each run, Pallas kernels for 0% -> 0%
where the time goes in v1:
time: 152 us
  waiting for transfers between devices  103 us (68%)
  Pallas kernels  20.6 us (14%)
  local copies, waits for them, and re-layouts  14.5 us (10%)
  between operations  13.8 us (9%)
    reduce_scatter x1, waiting for transfers between devices, body(): own_rows = lax.psum_scatter(gl, 'ctx', scatter_dimension=0, tiled=True)  43.8 us
    psum x1, waiting for transfers between devices, body(): return (out, gq, lax.psum(own_rows, 'head'))  35.5 us
    all_gather x1, waiting for transfers between devices, body(): all_lat = lax.all_gather(latents, 'ctx', axis=0, tiled=True)  23.9 us
    pallas_call x1, Pallas kernels, attention(): pl.pallas_call(functools.partial(attention_kernel, (n_ctx, half, heads, c...  20.6 us
    unnamed x12, local copies, waits for them, and re-layouts  14.5 us
  transfers between devices with their start and end apart: 3, of which 3 were waited for; matrix products, arithmetic and copies ran while one was open for 5% of the time, Pallas kernels for 0%

profile of v1, /device:TPU:0, one launch (start us, length us, event | category | flops | bytes accessed | tf_op | source)
XLA Modules:
  0.0 152.2 jit_solution(2600681759166118966)
XLA Ops:
  7.2 0.0 all-gather.2.cloned.1.call-start
  7.2 1.7 %copy.9 = bf16[128,576]{1,0:T(8,128)(2,1)} copy(bf16[128,576]{0,1:T(8,128)(2,1)} %param.6) | data formatting | bytes 294912 | tf_op args[1]
  8.9 0.0 all-gather.2.cloned.1.call-update
  8.9 0.0 copy-start.2
  9.0 0.0 copy-start.3
  9.0 0.0 reduce-scatter.2.cloned.1.call-start
  9.0 4.9 %copy.8 = bf16[128,16,576]{2,1,0:T(8,128)(2,1)} copy(bf16[128,16,576]{0,2,1:T(8,128)(2,1)} %param.5) | data formatting | bytes 4718592 | tf_op args[0]
  13.9 23.9 %all-gather.2.cloned.1.call-done.lat_ref = bf16[1024,576]{1,0:T(8,128)(2,1)} async-done(((bf16[128,576]{1,0:T(8,128)(2,1)}), bf16[1024,576]{1,0:T(8,128)(2,1)}) %all-gather.2.cloned.1.call-update) | async-done | bytes 1179664 | tf_op jit(solution)/shard_map/all_gather | solution.py:174
  37.8 0.0 copy-done.2
  37.8 0.0 copy-done.3
  37.8 0.0 copy-start
  37.8 1.6 %copy-done = bf16[128,16,512]{2,1,0:T(8,128)(2,1)S(1)} copy-done((bf16[128,16,512]{2,1,0:T(8,128)(2,1)S(1)}, bf16[128,16,512]{2,1,0:T(8,128)(2,1)}, u32[]{:S(2)}) %copy-start) | copy-done | bytes 2097176
  39.4 0.0 copy-start.1
  39.4 1.3 copy-done.1
  40.7 20.6 %shard_map.76 = (bf16[2048,512]{1,0:T(8,128)(2,1)}, bf16[2048,576]{1,0:T(8,128)(2,1)S(1)}, f32[1024,576]{1,0:T(8,128)}) custom-call(s32[8]{0:T(128)S(1)} %copy-done.3, s32[1024]{0:T(1024)S(1)} %copy-done.2, bf16[2048,576]{1,0:T(8,128)(2,1)} %bitcast.6, bf16[2048,512]{1,0:T(8,128)(2,1)S(1)} %bitcast.5, bf16[1024,576]{1,0:T(8,128)(2,1)S(1)} %copy-done.1), custom_call_target="tpu_custom_call" | custom-call | flops 7516192768 | bytes 12582912 | tf_op jit(solution)/shard_map/pallas_call | solution.py:135
  61.3 0.0 reduce-scatter.2.cloned.1.call-update
  61.4 0.0 all-reduce.2.cloned.1.call-start
  61.4 43.8 %reduce-scatter.2.cloned.1.call-done = f32[128,576]{1,0:T(8,128)} async-done(((f32[1024,576]{1,0:T(8,128)}), f32[128,576]{1,0:T(8,128)}) %reduce-scatter.2.cloned.1.call-update) | async-done | bytes 294928 | tf_op jit(solution)/shard_map/reduce_scatter | solution.py:176
  105.2 0.0 all-reduce.2.cloned.1.call-update
  105.2 3.1 %copy.10 = bf16[128,16,576]{0,2,1:T(8,128)(2,1)} copy(bf16[128,16,576]{2,1,0:T(8,128)(2,1)S(1)} %bitcast.4) | data formatting | bytes 4718592
  108.3 35.5 %all-reduce.2.cloned.1.call-done = f32[128,576]{1,0:T(8,128)} async-done(((f32[128,576]{1,0:T(8,128)}), f32[128,576]{1,0:T(8,128)}) %all-reduce.2.cloned.1.call-update) | async-done | bytes 294928 | tf_op jit(solution)/shard_map/psum | solution.py:177
  143.8 1.8 %copy.11 = f32[128,576]{0,1:T(8,128)} copy(f32[128,576]{1,0:T(8,128)} %all-reduce.2.cloned.1.call-done) | data formatting | bytes 589824
Async XLA Ops:
  7.2 30.6 %all-gather.2.cloned.1.call-start = ((), (), s32[]{:S(2)}) async-start(), calls=%async_computation.1 | async-start | bytes 1474560 | tf_op jit(solution)/shard_map/all_gather | solution.py:174
  8.9 28.8 %copy-start.2 = (s32[1024]{0:T(1024)S(1)}, s32[1024]{0:T(1024)}, u32[]{:S(2)}) copy-start(s32[1024]{0:T(1024)} %docs_ref.1) | copy-start | bytes 12292
  9.0 28.8 %copy-start.3 = (s32[8]{0:T(128)S(1)}, s32[8]{0:T(128)}, u32[]{:S(2)}) copy-start(s32[8]{0:T(128)} %order_ref.1) | copy-start | bytes 100
  9.0 96.2 %reduce-scatter.2.cloned.1.call-start = ((), (), s32[]{:S(2)}) async-start(), calls=%async_computation.2 | async-start | bytes 2949120 | tf_op jit(solution)/shard_map/reduce_scatter | solution.py:176
  37.8 1.6 %copy-start = (bf16[128,16,512]{2,1,0:T(8,128)(2,1)S(1)}, bf16[128,16,512]{2,1,0:T(8,128)(2,1)}, u32[]{:S(2)}) copy-start(bf16[128,16,512]{2,1,0:T(8,128)(2,1)} %param.7) | copy-start | bytes 6291460
  39.4 1.3 copy-start.1
  61.4 82.4 %all-reduce.2.cloned.1.call-start = ((), (), s32[]{:S(2)}) async-start(), calls=%async_computation.3 | async-start | bytes 655360 | tf_op jit(solution)/shard_map/psum | solution.py:177
Sparse Core Ops, SparseCore 0:
  10.5 27.2 all-gather.1
  61.5 43.6 reduce-scatter.1
  107.5 36.2 all-reduce.1

commit v2 on v1

--- a/solution.py
+++ b/solution.py
@@ -169,12 +169,168 @@
     return out.reshape(tok, heads, lat), gq.reshape(tok, heads, width), gl
 
 
+def transfer(src, dst, sems, index, device):
+    copy = pltpu.make_async_remote_copy(
+        src_ref=src, dst_ref=dst, send_sem=sems.at[0, index], recv_sem=sems.at[1, index],
+        device_id=device, device_id_type=pl.DeviceIdType.MESH,
+    )
+    copy.start()
+    return copy
+
+
+def greet(peers):
+    barrier = pltpu.get_barrier_semaphore()
+    for peer in peers:
+        pl.semaphore_signal(
+            barrier, inc=1, device_id=peer, device_id_type=pl.DeviceIdType.MESH
+        )
+    pl.semaphore_wait(barrier, len(peers))
+
+
+def places(n_ctx):
+    me = lax.axis_index("ctx")
+    core = lax.rem(me, 2)
+    chip = me // 2
+    sibling = chip * 2 + 1 - core
+    chips = n_ctx // 2
+    return me, core, chip, sibling, chips
+
+
+def gather_kernel(n_ctx, lat_ref, out_ref, own, sems, pair_sems, local_sem):
+    me, core, chip, sibling, chips = places(n_ctx)
+    z = lax.axis_index("head")
+    others = [lax.rem(chip + k, chips) * 2 + core for k in range(1, chips)]
+    greet([(sibling, z)] + [(other, z) for other in others])
+    own[...] = lat_ref[...].T
+    sends = [
+        transfer(own, out_ref.at[me], sems, k, (other, z)) for k, other in enumerate(others)
+    ]
+    pairs = [transfer(own, out_ref.at[me], pair_sems, 0, (sibling, z))]
+    keep = pltpu.make_async_copy(own, out_ref.at[me], local_sem)
+    keep.start()
+    for k in range(1, chips):
+        sends[k - 1].wait_recv()
+        owner = lax.rem(chip + chips - k, chips) * 2 + core
+        pairs.append(
+            transfer(out_ref.at[owner], out_ref.at[owner], pair_sems, k, (sibling, z))
+        )
+    for copy in sends:
+        copy.wait_send()
+    for copy in pairs:
+        copy.wait()
+    keep.wait()
+
+
+def gather(latents, n_ctx):
+    tok, width = latents.shape
+    out = pl.pallas_call(
+        functools.partial(gather_kernel, n_ctx),
+        in_specs=[pl.BlockSpec(memory_space=pltpu.VMEM)],
+        out_specs=pl.BlockSpec(memory_space=pl.ANY),
+        out_shape=jax.ShapeDtypeStruct((n_ctx, tok, width), latents.dtype),
+        scratch_shapes=[
+            pltpu.VMEM((tok, width), latents.dtype),
+            pltpu.SemaphoreType.DMA((2, n_ctx // 2)),
+            pltpu.SemaphoreType.DMA((2, n_ctx // 2)),
+            pltpu.SemaphoreType.DMA,
+        ],
+        compiler_params=pltpu.CompilerParams(collective_id=0, has_side_effects=True),
+    )(latents.T)
+    return out.reshape(n_ctx * tok, width)
+
+
+def reduce_kernel(
+    n_ctx, n_head, part_ref, out_ref, pair_in, chip_out, chip_in, head_out, head_in, whole,
+    pair_sems, chip_sems, head_sems, last_sems,
+):
+    me, core, chip, sibling, chips = places(n_ctx)
+    z = lax.axis_index("head")
+    others = [lax.rem(chip + k, chips) * 2 + core for k in range(1, chips)]
+    heads = [lax.rem(z + k, n_head) for k in range(1, n_head)]
+    greet(
+        [(sibling, z)] + [(other, z) for other in others] + [(me, other) for other in heads]
+    )
+    order = [lax.rem(chip + k, chips) for k in range(1, chips + 1)]
+    pairs = [
+        transfer(
+            part_ref.at[target * 2 + 1 - core], pair_in.at[k], pair_sems, k, (sibling, z)
+        )
+        for k, target in enumerate(order)
+    ]
+    sends = []
+    total = None
+    for k, target in enumerate(order):
+        pairs[k].wait_recv()
+        total = part_ref[target * 2 + core].astype(jnp.float32) + pair_in[k].astype(jnp.float32)
+        if k < chips - 1:
+            chip_out[k] = total.astype(jnp.bfloat16)
+            sends.append(
+                transfer(chip_out.at[k], chip_in.at[k], chip_sems, k, (others[k], z))
+            )
+    for k, copy in enumerate(sends):
+        copy.wait_recv()
+        total = total + chip_in[k].astype(jnp.float32)
+    rows = total.shape[0] // n_head
+    for k in range(n_head):
+        head_out[k] = total[k * rows : (k + 1) * rows].astype(jnp.bfloat16)
+    steps = [
+        transfer(head_out.at[other], head_in.at[k], head_sems, k, (me, other))
+        for k, other in enumerate(heads)
+    ]
+    piece = head_out[z].astype(jnp.float32)
+    for k, copy in enumerate(steps):
+        copy.wait_recv()
+        piece = piece + head_in[k].astype(jnp.float32)
+    whole[z] = piece.astype(jnp.bfloat16)
+    lasts = [
+        transfer(whole.at[z], whole.at[z], last_sems, k, (me, other))
+        for k, other in enumerate(heads)
+    ]
+    for copy in lasts:
+        copy.wait_recv()
+    result = jnp.concatenate([whole[k] for k in range(n_head)], axis=0)
+    out_ref[...] = result.astype(jnp.float32).T
+    for copy in pairs + sends + steps + lasts:
+        copy.wait_send()
+
+
+def reduce_parts(parts, n_ctx, n_head):
+    seq, width = parts.shape
+    tok = seq // n_ctx
+    rows = tok // n_head
+    chips = n_ctx // 2
+    kind = parts.dtype
+    vmem = pl.BlockSpec(memory_space=pltpu.VMEM)
+    out = pl.pallas_call(
+        functools.partial(reduce_kernel, n_ctx, n_head),
+        in_specs=[vmem],
+        out_specs=vmem,
+        out_shape=jax.ShapeDtypeStruct((width, tok), jnp.float32),
+        scratch_shapes=[
+            pltpu.VMEM((chips, tok, width), kind),
+            pltpu.VMEM((chips, tok, width), kind),
+            pltpu.VMEM((chips, tok, width), kind),
+            pltpu.VMEM((n_head, rows, width), kind),
+            pltpu.VMEM((n_head, rows, width), kind),
+            pltpu.VMEM((n_head, rows, width), kind),
+            pltpu.SemaphoreType.DMA((2, chips)),
+            pltpu.SemaphoreType.DMA((2, chips)),
+            pltpu.SemaphoreType.DMA((2, n_head)),
+            pltpu.SemaphoreType.DMA((2, n_head)),
+        ],
+        compiler_params=pltpu.CompilerParams(
+            collective_id=1, has_side_effects=True, vmem_limit_bytes=32 * 1024 * 1024
+        ),
+    )(parts.reshape(n_ctx, tok, width))
+    return out.T
+
+
 def body(queries, latents, grad_out, block_order, doc_ids):
     n_ctx = lax.axis_size("ctx")
-    all_lat = lax.all_gather(latents, "ctx", axis=0, tiled=True)
-    out, gq, gl = attention(queries, grad_out, all_lat, block_order, doc_ids, n_ctx, jnp.float32)
-    own_rows = lax.psum_scatter(gl, "ctx", scatter_dimension=0, tiled=True)
-    return out, gq, lax.psum(own_rows, "head")
+    n_head = lax.axis_size("head")
+    all_lat = gather(latents, n_ctx)
+    out, gq, gl = attention(queries, grad_out, all_lat, block_order, doc_ids, n_ctx, jnp.bfloat16)
+    return out, gq, reduce_parts(gl, n_ctx, n_head)
 
 
 def solution(mesh):

time: 152 us -> 72.4 us (0.48)
  waiting for transfers between devices: 103 us -> 0 us
  Pallas kernels: 20.6 us -> 58.3 us
  between operations: 13.8 us -> 0.69 us
  local copies, waits for them, and re-layouts: 14.5 us -> 12 us
    reduce_scatter x1 -> x0, waiting for transfers between devices: 43.8 us -> none  [body(): own_rows = lax.psum_scatter(gl, 'ctx', scatter_dimension=0, tiled=True)]
    pallas_call x0 -> x2, Pallas kernels: none -> 42.3 us  [the longest x1 27.6 us: reduce_parts(): pl.pallas_call(functools.partial(reduce_kernel, n_ctx, n_head), in_specs=...]
    psum x1 -> x0, waiting for transfers between devices: 35.5 us -> none  [body(): return (out, gq, lax.psum(own_rows, 'head'))]
    all_gather x1 -> x0, waiting for transfers between devices: 23.9 us -> none  [body(): all_lat = lax.all_gather(latents, 'ctx', axis=0, tiled=True)]
    pallas_call x1, Pallas kernels: 20.6 us -> 16 us  [attention(): pl.pallas_call(functools.partial(attention_kernel, (n_ctx, half, heads, c...]
    unnamed x12 -> x11, local copies, waits for them, and re-layouts: 14.5 us -> 12 us
  transfers between devices with their start and end apart: 3 -> 0, of which waited for: 3 -> 0; matrix products, arithmetic and copies ran while one was open for 5% -> 0% of each run, Pallas kernels for 0% -> 0%
where the time goes in v2:
time: 72.4 us; the launch traced here: 71 us
  Pallas kernels  58.3 us (81%)
  local copies, waits for them, and re-layouts  12 us (17%)
    pallas_call x1, Pallas kernels, reduce_parts(): pl.pallas_call(functools.partial(reduce_kernel, n_ctx, n_head), in_specs=...  27.6 us
    pallas_call x1, Pallas kernels, attention(): pl.pallas_call(functools.partial(attention_kernel, (n_ctx, half, heads, c...  16 us
    pallas_call x1, Pallas kernels, gather(): pl.pallas_call(functools.partial(gather_kernel, n_ctx), in_specs=[pl.Bloc...  14.8 us
    unnamed x11, local copies, waits for them, and re-layouts  12 us

profile of v2, /device:TPU:0, one launch (start us, length us, event | category | flops | bytes accessed | tf_op | source)
XLA Modules:
  0.0 71.0 jit_solution(16207960395663501369)
XLA Ops:
  0.6 14.8 %shard_map.76 = bf16[8,128,576]{2,1,0:T(8,128)(2,1)} custom-call(bf16[576,128]{1,0:T(8,128)(2,1)} %bitcast.14), custom_call_target="tpu_custom_call" | custom-call | tf_op jit(solution)/shard_map/pallas_call | solution.py:226
  15.4 0.0 copy-start
  15.4 0.0 copy-start.2
  15.4 0.0 copy-start.3
  15.4 5.0 %copy.8 = bf16[128,16,576]{2,1,0:T(8,128)(2,1)} copy(bf16[128,16,576]{0,2,1:T(8,128)(2,1)} %param.5) | data formatting | bytes 4718592 | tf_op args[0]
  20.5 0.0 copy-done
  20.5 0.0 copy-done.2
  20.5 0.0 copy-done.3
  20.5 0.0 copy-start.1
  20.5 1.6 %copy-done.1 = bf16[128,16,512]{2,1,0:T(8,128)(2,1)S(1)} copy-done((bf16[128,16,512]{2,1,0:T(8,128)(2,1)S(1)}, bf16[128,16,512]{2,1,0:T(8,128)(2,1)}, u32[]{:S(2)}) %copy-start.1) | copy-done | bytes 2097176
  22.1 16.0 %shard_map.77 = (bf16[2048,512]{1,0:T(8,128)(2,1)}, bf16[2048,576]{1,0:T(8,128)(2,1)}, bf16[1024,576]{1,0:T(8,128)(2,1)S(1)}) custom-call(s32[8]{0:T(128)S(1)} %copy-done.3, s32[1024]{0:T(1024)S(1)} %copy-done.2, bf16[2048,576]{1,0:T(8,128)(2,1)} %bitcast.13, bf16[2048,512]{1,0:T(8,128)(2,1)S(1)} %bitcast.11, bf16[1024,576]{1,0:T(8,128)(2,1)S(1)} %bitcast.9), custom_call_target="tpu_custom_call" | custom-call | flops 7516192768 | bytes 12582912 | tf_op jit(solution)/shard_map/pallas_call | solution.py:135
  38.1 4.7 %copy.9 = bf16[128,16,576]{0,2,1:T(8,128)(2,1)} copy(bf16[128,16,576]{2,1,0:T(8,128)(2,1)} %bitcast.12) | data formatting | bytes 4718592
  42.8 27.6 %shard_map.78 = f32[576,128]{1,0:T(8,128)S(1)} custom-call(bf16[8,128,576]{2,1,0:T(8,128)(2,1)S(1)} %bitcast.8), custom_call_target="tpu_custom_call" | custom-call | tf_op jit(solution)/shard_map/pallas_call | solution.py:304
  70.3 0.7 %copy.11 = f32[128,576]{0,1:T(8,128)} copy(f32[128,576]{0,1:T(8,128)S(1)} %bitcast.10) | data formatting | bytes 589824
Async XLA Ops:
  15.4 5.1 %copy-start = (bf16[8,128,576]{2,1,0:T(8,128)(2,1)S(1)}, bf16[8,128,576]{2,1,0:T(8,128)(2,1)}, u32[]{:S(2)}) copy-start(bf16[8,128,576]{2,1,0:T(8,128)(2,1)} %shard_map.76) | copy-start | bytes 3538948
  15.4 5.0 %copy-start.2 = (s32[1024]{0:T(1024)S(1)}, s32[1024]{0:T(1024)}, u32[]{:S(2)}) copy-start(s32[1024]{0:T(1024)} %docs_ref.1) | copy-start | bytes 12292
  15.4 5.0 %copy-start.3 = (s32[8]{0:T(128)S(1)}, s32[8]{0:T(128)}, u32[]{:S(2)}) copy-start(s32[8]{0:T(128)} %order_ref.1) | copy-start | bytes 100
  20.5 1.6 %copy-start.1 = (bf16[128,16,512]{2,1,0:T(8,128)(2,1)S(1)}, bf16[128,16,512]{2,1,0:T(8,128)(2,1)}, u32[]{:S(2)}) copy-start(bf16[128,16,512]{2,1,0:T(8,128)(2,1)} %param.7) | copy-start | bytes 6291460

commit v3 on v2

--- a/solution.py
+++ b/solution.py
@@ -11,7 +11,8 @@
 far_below = -1e30
 DOCS = 4
 KEY_TILE = 256
-ROWS = 512
+COLS = 512
+LANES = 128
 NT = (((1,), (1,)), ((), ()))
 NN = (((1,), (0,)), ((), ()))
 TN = (((0,), (0,)), ((), ()))
@@ -23,18 +24,18 @@
 
 def attention_kernel(
     shape, order_ref, docs_ref, q_ref, g_ref, lat_ref, out_ref, gq_ref, gl_ref,
-    keys, grad_keys, scores, acc, acc_q, bounds, sems,
+    keys, grad_keys, scores, grad_probs, out_acc, q_acc, by_token, bounds, sems,
 ):
-    n_ctx, half, heads, chunk_tok, lat = shape
+    n_ctx, half, heads, cols, lat = shape
     seq = 2 * half * n_ctx
-    c = pl.program_id(0)
+    part = pl.program_id(0)
     me = lax.axis_index("ctx")
 
     def block_of(slot):
         low = order_ref[slot // 2]
         return low if slot % 2 == 0 else 2 * n_ctx - 1 - low
 
-    @pl.when(c == 0)
+    @pl.when(part == 0)
     def _():
         copies = []
         for slot in range(2 * n_ctx):
@@ -58,63 +59,91 @@
             copy.wait()
 
     low = order_ref[me]
-    first_tok = c * chunk_tok
-    block = jnp.where(first_tok < half, low, 2 * n_ctx - 1 - low)
-    pos0 = block * half + lax.rem(first_tok, half)
+    pos0 = jnp.where(part == 0, low, 2 * n_ctx - 1 - low) * half
     doc_start = jnp.int32(0)
     for number in range(1, DOCS):
         doc_start = jnp.where(bounds[number] <= pos0, bounds[number], doc_start)
     start = (doc_start // 16) * 16
-    tiles = (pos0 + chunk_tok - start + KEY_TILE - 1) // KEY_TILE
-
-    rows = chunk_tok * heads
-    row_pos = pos0 + lax.broadcasted_iota(jnp.int32, (rows, 1), 0) // heads
+    tiles = (pos0 + half - start + KEY_TILE - 1) // KEY_TILE
+
+    row_pos = pos0 + lax.rem(lax.broadcasted_iota(jnp.int32, (1, cols), 1), half)
     row_doc = jnp.zeros_like(row_pos)
     for number in range(1, DOCS):
         row_doc = jnp.where(bounds[number] <= row_pos, bounds[number], row_doc)
-    q = q_ref[...]
-    g = g_ref[...]
 
     def tile_at(i):
         return pl.ds(pl.multiple_of(start + i * KEY_TILE, 16), KEY_TILE)
 
-    def first_pass(i, row_max):
-        s = dot(q, keys[tile_at(i), :], NT) * score_scale
-        key_pos = start + i * KEY_TILE + lax.broadcasted_iota(jnp.int32, (1, KEY_TILE), 1)
-        s = jnp.where((key_pos <= row_pos) & (key_pos >= row_doc), s, far_below)
-        scores[i] = s
-        return jnp.maximum(row_max, jnp.max(s, axis=1, keepdims=True))
-
-    row_max = lax.fori_loop(0, tiles, first_pass, jnp.full((rows, 1), far_below, jnp.float32))
-    acc[...] = jnp.zeros_like(acc)
-
-    def second_pass(i, row_sum):
-        e = jnp.exp(scores[i] - row_max)
-        scores[i] = e
-        acc[...] += dot(e.astype(jnp.bfloat16), keys[tile_at(i), :lat], NN)
-        return row_sum + jnp.sum(e, axis=1, keepdims=True)
-
-    row_sum = lax.fori_loop(0, tiles, second_pass, jnp.zeros((rows, 1), jnp.float32))
-    inverse = 1.0 / row_sum
-    out = (acc[...] * inverse).astype(jnp.bfloat16)
-    out_ref[...] = out
-    delta = jnp.sum(g.astype(jnp.float32) * out.astype(jnp.float32), axis=1, keepdims=True)
-    acc_q[...] = jnp.zeros_like(acc_q)
-
-    def third_pass(i, carry):
-        at = tile_at(i)
-        grad_probs = dot(g, keys[at, :lat], NT)
-        probs = scores[i] * inverse
-        ds = (probs * (grad_probs - delta) * score_scale).astype(jnp.bfloat16)
-        acc_q[...] += dot(ds, keys[at, :], NN)
-        grad_keys[at, :] += dot(ds, q, TN)
-        grad_keys[at, :lat] += dot(probs.astype(jnp.bfloat16), g, TN)
-        return carry
-
-    lax.fori_loop(0, tiles, third_pass, 0)
-    gq_ref[...] = acc_q[...].astype(jnp.bfloat16)
-
-    @pl.when(c == pl.num_programs(0) - 1)
+    heads_now = cols // half
+    for chunk in range(heads * half // cols):
+        here = slice(chunk * cols, (chunk + 1) * cols)
+
+        def first_pass(i, row_max):
+            at = tile_at(i)
+            s = dot(keys[at, :], q_ref[0, :, here], NN) * score_scale
+            key_pos = start + i * KEY_TILE + lax.broadcasted_iota(jnp.int32, (KEY_TILE, 1), 0)
+            s = jnp.where((key_pos <= row_pos) & (key_pos >= row_doc), s, far_below)
+            scores[i] = s
+            grad_probs[i] = dot(keys[at, :lat], g_ref[0, here, :], NT)
+            return jnp.maximum(row_max, jnp.max(s, axis=0, keepdims=True))
+
+        row_max = lax.fori_loop(
+            0, tiles, first_pass, jnp.full((1, cols), far_below, jnp.float32)
+        )
+
+        def second_pass(i, sums):
+            row_sum, weighted = sums
+            e = jnp.exp(scores[i] - row_max)
+            scores[i] = e
+            return (
+                row_sum + jnp.sum(e, axis=0, keepdims=True),
+                weighted + jnp.sum(e * grad_probs[i], axis=0, keepdims=True),
+            )
+
+        zero = jnp.zeros((1, cols), jnp.float32)
+        row_sum, weighted = lax.fori_loop(0, tiles, second_pass, (zero, zero))
+        inverse = 1.0 / row_sum
+        delta = weighted * inverse
+        scaled = inverse * score_scale
+        out_acc[...] = jnp.zeros_like(out_acc)
+        q_acc[...] = jnp.zeros_like(q_acc)
+
+        def third_pass(i, carry):
+            at = tile_at(i)
+            e = scores[i]
+            probs = (e * inverse).astype(jnp.bfloat16)
+            ds = (e * scaled * (grad_probs[i] - delta)).astype(jnp.bfloat16)
+            out_acc[...] += dot(probs, keys[at, :lat], TN)
+            q_acc[...] += dot(keys[at, :], ds, TN)
+            key_term = dot(ds, q_ref[0, :, here], NT)
+            value_term = dot(probs, g_ref[0, here, :], NN)
+            grad_keys[at, :lat] += key_term[:, :lat] + value_term
+            grad_keys[at, lat:] += key_term[:, lat:]
+            return carry
+
+        lax.fori_loop(0, tiles, third_pass, 0)
+        for k in range(heads_now):
+            head = chunk * heads_now + k
+            mine = slice(k * half, (k + 1) * half)
+            for lanes in range(lat // LANES):
+                by_token[lanes, pl.ds(head, half, stride=heads), :] = out_acc[
+                    mine, lanes * LANES : (lanes + 1) * LANES
+                ]
+
+        for p in range(2):
+            @pl.when(part == p)
+            def _():
+                for k in range(heads_now):
+                    head = chunk * heads_now + k
+                    mine = slice(k * half, (k + 1) * half)
+                    gq_ref[head, :, p * half : (p + 1) * half] = q_acc[:, mine].astype(
+                        gq_ref.dtype
+                    )
+
+    for lanes in range(lat // LANES):
+        out_ref[:, lanes * LANES : (lanes + 1) * LANES] = by_token[lanes].astype(out_ref.dtype)
+
+    @pl.when(part == 1)
     def _():
         for slot in range(2 * n_ctx):
             first = pl.multiple_of(block_of(slot) * half, half)
@@ -123,50 +152,51 @@
             )
 
 
-def attention(queries, grad_out, all_lat, block_order, doc_ids, n_ctx, sum_type):
-    tok, heads, width = queries.shape
-    lat = grad_out.shape[2]
-    half = tok // 2
+def attention(q_cols, g_rows, all_lat, block_order, doc_ids, n_ctx, heads):
+    width, total = q_cols.shape[1:]
+    lat = g_rows.shape[2]
+    half = total // heads
+    tok = 2 * half
     seq = tok * n_ctx
-    chunk_tok = min(half, max(1, ROWS // heads))
-    rows = chunk_tok * heads
+    cols = min(total, COLS)
     tile_count = seq // KEY_TILE + 1
-    block = lambda w: pl.BlockSpec((rows, w), lambda c, *_: (c, 0))
-    out, gq, gl = pl.pallas_call(
-        functools.partial(attention_kernel, (n_ctx, half, heads, chunk_tok, lat)),
+    return pl.pallas_call(
+        functools.partial(attention_kernel, (n_ctx, half, heads, cols, lat)),
         grid_spec=pltpu.PrefetchScalarGridSpec(
             num_scalar_prefetch=2,
-            grid=(tok // chunk_tok,),
-            in_specs=[block(width), block(lat), pl.BlockSpec(memory_space=pl.ANY)],
+            grid=(2,),
+            in_specs=[
+                pl.BlockSpec((1, width, total), lambda p, *_: (p, 0, 0)),
+                pl.BlockSpec((1, total, lat), lambda p, *_: (p, 0, 0)),
+                pl.BlockSpec(memory_space=pl.ANY),
+            ],
             out_specs=[
-                block(lat),
-                block(width),
-                pl.BlockSpec((seq, width), lambda c, *_: (0, 0)),
+                pl.BlockSpec((total, lat), lambda p, *_: (p, 0)),
+                pl.BlockSpec((heads, width, tok), lambda p, *_: (0, 0, 0)),
+                pl.BlockSpec((seq, width), lambda p, *_: (0, 0)),
             ],
             scratch_shapes=[
                 pltpu.VMEM((seq + KEY_TILE, width), jnp.bfloat16),
                 pltpu.VMEM((seq + KEY_TILE, width), jnp.float32),
-                pltpu.VMEM((tile_count, rows, KEY_TILE), jnp.float32),
-                pltpu.VMEM((rows, lat), jnp.float32),
-                pltpu.VMEM((rows, width), jnp.float32),
+                pltpu.VMEM((tile_count, KEY_TILE, cols), jnp.float32),
+                pltpu.VMEM((tile_count, KEY_TILE, cols), jnp.float32),
+                pltpu.VMEM((cols, lat), jnp.float32),
+                pltpu.VMEM((width, cols), jnp.float32),
+                pltpu.VMEM((lat // LANES, total, LANES), jnp.float32),
                 pltpu.SMEM((DOCS,), jnp.int32),
                 pltpu.SemaphoreType.DMA((2 * n_ctx,)),
             ],
         ),
         out_shape=[
             jax.ShapeDtypeStruct((tok * heads, lat), jnp.bfloat16),
-            jax.ShapeDtypeStruct((tok * heads, width), jnp.bfloat16),
-            jax.ShapeDtypeStruct((seq, width), sum_type),
+            jax.ShapeDtypeStruct((heads, width, tok), jnp.bfloat16),
+            jax.ShapeDtypeStruct((seq, width), jnp.bfloat16),
         ],
         compiler_params=pltpu.CompilerParams(vmem_limit_bytes=48 * 1024 * 1024),
         cost_estimate=pl.CostEstimate(
             flops=14 * tok * heads * seq * lat // 2, bytes_accessed=12 << 20, transcendentals=0
         ),
-    )(
-        block_order, doc_ids,
-        queries.reshape(tok * heads, width), grad_out.reshape(tok * heads, lat), all_lat,
-    )
-    return out.reshape(tok, heads, lat), gq.reshape(tok, heads, width), gl
+    )(block_order, doc_ids, q_cols, g_rows, all_lat)
 
 
 def transfer(src, dst, sems, index, device):
@@ -196,18 +226,50 @@
     return me, core, chip, sibling, chips
 
 
-def gather_kernel(n_ctx, lat_ref, out_ref, own, sems, pair_sems, local_sem):
+def gather_kernel(
+    n_ctx, lat_ref, q_hbm, g_hbm, out_ref, q_out, g_out, own, q_in, g_in, g_wide,
+    sems, pair_sems, local_sems,
+):
     me, core, chip, sibling, chips = places(n_ctx)
     z = lax.axis_index("head")
     others = [lax.rem(chip + k, chips) * 2 + core for k in range(1, chips)]
+    loads = [
+        pltpu.make_async_copy(q_hbm, q_in, local_sems.at[0]),
+        pltpu.make_async_copy(g_hbm, g_in, local_sems.at[1]),
+    ]
+    for load in loads:
+        load.start()
+    own[...] = lat_ref[...].T
     greet([(sibling, z)] + [(other, z) for other in others])
-    own[...] = lat_ref[...].T
     sends = [
         transfer(own, out_ref.at[me], sems, k, (other, z)) for k, other in enumerate(others)
     ]
     pairs = [transfer(own, out_ref.at[me], pair_sems, 0, (sibling, z))]
-    keep = pltpu.make_async_copy(own, out_ref.at[me], local_sem)
+    keep = pltpu.make_async_copy(own, out_ref.at[me], local_sems.at[2])
     keep.start()
+
+    heads, width, tok = q_in.shape
+    half = tok // 2
+    loads[0].wait()
+
+    def pack_heads(k, carry):
+        a, b = q_in[2 * k], q_in[2 * k + 1]
+        at = pl.ds(pl.multiple_of(k * tok, tok), tok)
+        q_out[0, :, at] = jnp.concatenate([a[:, :half], b[:, :half]], axis=1)
+        q_out[1, :, at] = jnp.concatenate([a[:, half:], b[:, half:]], axis=1)
+        return carry
+
+    lax.fori_loop(0, heads // 2, pack_heads, 0)
+    loads[1].wait()
+    for p in range(2):
+        for lanes in range(g_wide.shape[0]):
+            at = slice(lanes * LANES, (lanes + 1) * LANES)
+            g_wide[lanes] = g_in[p * half * heads : (p + 1) * half * heads, at].astype(jnp.float32)
+            for head in range(heads):
+                g_out[p, head * half : (head + 1) * half, at] = g_wide[
+                    lanes, pl.ds(head, half, stride=heads), :
+                ].astype(g_out.dtype)
+
     for k in range(1, chips):
         sends[k - 1].wait_recv()
         owner = lax.rem(chip + chips - k, chips) * 2 + core
@@ -221,22 +283,36 @@
     keep.wait()
 
 
-def gather(latents, n_ctx):
+def gather(latents, queries, grad_out, n_ctx):
     tok, width = latents.shape
-    out = pl.pallas_call(
+    heads, lat = grad_out.shape[1:]
+    total = heads * tok // 2
+    vmem = pl.BlockSpec(memory_space=pltpu.VMEM)
+    hbm = pl.BlockSpec(memory_space=pl.ANY)
+    kind = latents.dtype
+    out, q_cols, g_rows = pl.pallas_call(
         functools.partial(gather_kernel, n_ctx),
-        in_specs=[pl.BlockSpec(memory_space=pltpu.VMEM)],
-        out_specs=pl.BlockSpec(memory_space=pl.ANY),
-        out_shape=jax.ShapeDtypeStruct((n_ctx, tok, width), latents.dtype),
+        in_specs=[vmem, hbm, hbm],
+        out_specs=[hbm, vmem, vmem],
+        out_shape=[
+            jax.ShapeDtypeStruct((n_ctx, tok, width), kind),
+            jax.ShapeDtypeStruct((2, width, total), kind),
+            jax.ShapeDtypeStruct((2, total, lat), kind),
+        ],
         scratch_shapes=[
-            pltpu.VMEM((tok, width), latents.dtype),
+            pltpu.VMEM((tok, width), kind),
+            pltpu.VMEM((heads, width, tok), kind),
+            pltpu.VMEM((tok * heads, lat), kind),
+            pltpu.VMEM((lat // LANES, total, LANES), jnp.float32),
             pltpu.SemaphoreType.DMA((2, n_ctx // 2)),
             pltpu.SemaphoreType.DMA((2, n_ctx // 2)),
-            pltpu.SemaphoreType.DMA,
+            pltpu.SemaphoreType.DMA((3,)),
         ],
-        compiler_params=pltpu.CompilerParams(collective_id=0, has_side_effects=True),
-    )(latents.T)
-    return out.reshape(n_ctx * tok, width)
+        compiler_params=pltpu.CompilerParams(
+            collective_id=0, has_side_effects=True, vmem_limit_bytes=32 * 1024 * 1024
+        ),
+    )(latents.T, jnp.transpose(queries, (1, 2, 0)), grad_out.reshape(tok * heads, lat))
+    return out.reshape(n_ctx * tok, width), q_cols, g_rows
 
 
 def reduce_kernel(
@@ -328,9 +404,11 @@
 def body(queries, latents, grad_out, block_order, doc_ids):
     n_ctx = lax.axis_size("ctx")
     n_head = lax.axis_size("head")
-    all_lat = gather(latents, n_ctx)
-    out, gq, gl = attention(queries, grad_out, all_lat, block_order, doc_ids, n_ctx, jnp.bfloat16)
-    return out, gq, reduce_parts(gl, n_ctx, n_head)
+    tok, heads, lat = grad_out.shape
+    all_lat, q_cols, g_rows = gather(latents, queries, grad_out, n_ctx)
+    out, gq, gl = attention(q_cols, g_rows, all_lat, block_order, doc_ids, n_ctx, heads)
+    grad_latents = reduce_parts(gl, n_ctx, n_head)
+    return out.reshape(tok, heads, lat), jnp.transpose(gq, (2, 0, 1)), grad_latents
 
 
 def solution(mesh):

time: 72.4 us -> 64.1 us (0.89); the launches traced: 71 us -> 64.2 us
  local copies, waits for them, and re-layouts: 12 us -> 6.28 us
  Pallas kernels: 58.3 us -> 57.3 us
    unnamed x11 -> x13, local copies, waits for them, and re-layouts: 12 us -> 6.28 us
    pallas_call x1, Pallas kernels: 14.8 us -> 13.7 us  [gather(): pl.pallas_call(functools.partial(gather_kernel, n_ctx), in_specs=[vmem, h...]
where the time goes in v3:
time: 64.1 us; the launch traced here: 64.2 us
  Pallas kernels  57.3 us (89%)
  local copies, waits for them, and re-layouts  6.28 us (10%)
  between operations  0.68 us (1%)
    pallas_call x1, Pallas kernels, reduce_parts(): pl.pallas_call(functools.partial(reduce_kernel, n_ctx, n_head), in_specs=...  27 us
    pallas_call x1, Pallas kernels, attention(): pl.pallas_call(functools.partial(attention_kernel, (n_ctx, half, heads, c...  16.6 us
    pallas_call x1, Pallas kernels, gather(): pl.pallas_call(functools.partial(gather_kernel, n_ctx), in_specs=[vmem, h...  13.7 us
    unnamed x13, local copies, waits for them, and re-layouts  6.28 us

profile of v3, /device:TPU:0, one launch (start us, length us, event | category | flops | bytes accessed | tf_op | source)
XLA Modules:
  0.0 64.2 jit_solution(8637837754006667786)
XLA Ops:
  0.6 0.0 copy-start
  0.6 1.7 %copy-done = bf16[128,16,576]{0,2,1:T(8,128)(2,1)S(1)} copy-done((bf16[128,16,576]{0,2,1:T(8,128)(2,1)S(1)}, bf16[128,16,576]{0,2,1:T(8,128)(2,1)}, u32[]{:S(2)}) %copy-start) | copy-done | bytes 2359320
  2.3 0.0 copy-start.1
  2.3 1.6 %copy-done.1 = bf16[128,16,512]{2,1,0:T(8,128)(2,1)S(1)} copy-done((bf16[128,16,512]{2,1,0:T(8,128)(2,1)S(1)}, bf16[128,16,512]{2,1,0:T(8,128)(2,1)}, u32[]{:S(2)}) %copy-start.1) | copy-done | bytes 2097176
  3.9 0.0 copy-start.2
  3.9 0.9 %copy-done.2 = bf16[128,576]{0,1:T(8,128)(2,1)S(1)} copy-done((bf16[128,576]{0,1:T(8,128)(2,1)S(1)}, bf16[128,576]{0,1:T(8,128)(2,1)}, u32[]{:S(2)}) %copy-start.2) | copy-done | bytes 147480
  4.8 0.0 copy-start.4
  4.8 0.0 copy-start.5
  4.8 13.7 %shard_map.76 = (bf16[8,128,576]{2,1,0:T(8,128)(2,1)S(1)}, bf16[2,576,1024]{2,1,0:T(8,128)(2,1)S(1)}, bf16[2,1024,512]{2,1,0:T(8,128)(2,1)S(1)}) custom-call(bf16[576,128]{1,0:T(8,128)(2,1)S(1)} %bitcast.12, bf16[16,576,128]{2,1,0:T(8,128)(2,1)S(1)} %bitcast.8, bf16[2048,512]{1,0:T(8,128)(2,1)S(1)} %bitcast.9), custom_call_target="tpu_custom_call" | custom-call | tf_op jit(solution)/shard_map/pallas_call | solution.py:293
  18.5 0.0 copy-start.3
  18.5 1.4 %copy-done.3 = bf16[2,576,1024]{2,1,0:T(8,128)(2,1)} copy-done((bf16[2,576,1024]{2,1,0:T(8,128)(2,1)}, bf16[2,576,1024]{2,1,0:T(8,128)(2,1)S(1)}, u32[]{:S(2)}) %copy-start.3) | copy-done | bytes 2359320
  19.9 0.0 copy-done.4
  19.9 0.0 copy-done.5
  19.9 16.6 %shard_map.77 = (bf16[2048,512]{1,0:T(8,128)(2,1)}, bf16[16,576,128]{2,1,0:T(8,128)(2,1)}, bf16[1024,576]{1,0:T(8,128)(2,1)S(1)}) custom-call(s32[8]{0:T(128)S(1)} %copy-done.5, s32[1024]{0:T(1024)S(1)} %copy-done.4, bf16[2,576,1024]{2,1,0:T(8,128)(2,1)} %copy-done.3, bf16[2,1024,512]{2,1,0:T(8,128)(2,1)S(1)} %get-tuple-element.10.g_ref, ...), custom_call_target="tpu_custom_call" | custom-call | flops 7516192768 | bytes 12582912 | tf_op jit(solution)/shard_map/pallas_call | solution.py:163
  36.5 27.0 %shard_map.78 = f32[576,128]{1,0:T(8,128)S(1)} custom-call(bf16[8,128,576]{2,1,0:T(8,128)(2,1)S(1)} %bitcast.10), custom_call_target="tpu_custom_call" | custom-call | tf_op jit(solution)/shard_map/pallas_call | solution.py:380
  63.5 0.7 %copy.9 = f32[128,576]{0,1:T(8,128)} copy(f32[128,576]{0,1:T(8,128)S(1)} %bitcast.11) | data formatting | bytes 589824
Async XLA Ops:
  0.6 1.7 %copy-start = (bf16[128,16,576]{0,2,1:T(8,128)(2,1)S(1)}, bf16[128,16,576]{0,2,1:T(8,128)(2,1)}, u32[]{:S(2)}) copy-start(bf16[128,16,576]{0,2,1:T(8,128)(2,1)} %param.5) | copy-start | bytes 7077892
  2.3 1.6 %copy-start.1 = (bf16[128,16,512]{2,1,0:T(8,128)(2,1)S(1)}, bf16[128,16,512]{2,1,0:T(8,128)(2,1)}, u32[]{:S(2)}) copy-start(bf16[128,16,512]{2,1,0:T(8,128)(2,1)} %param.7) | copy-start | bytes 6291460
  3.9 0.9 %copy-start.2 = (bf16[128,576]{0,1:T(8,128)(2,1)S(1)}, bf16[128,576]{0,1:T(8,128)(2,1)}, u32[]{:S(2)}) copy-start(bf16[128,576]{0,1:T(8,128)(2,1)} %param.6) | copy-start | bytes 442372
  4.8 15.1 %copy-start.4 = (s32[1024]{0:T(1024)S(1)}, s32[1024]{0:T(1024)}, u32[]{:S(2)}) copy-start(s32[1024]{0:T(1024)} %docs_ref.1) | copy-start | bytes 12292
  4.8 15.1 %copy-start.5 = (s32[8]{0:T(128)S(1)}, s32[8]{0:T(128)}, u32[]{:S(2)}) copy-start(s32[8]{0:T(128)} %order_ref.1) | copy-start | bytes 100
  18.5 1.4 %copy-start.3 = (bf16[2,576,1024]{2,1,0:T(8,128)(2,1)}, bf16[2,576,1024]{2,1,0:T(8,128)(2,1)S(1)}, u32[]{:S(2)}) copy-start(bf16[2,576,1024]{2,1,0:T(8,128)(2,1)S(1)} %get-tuple-element.9.q_ref) | copy-start | bytes 7077892

commit v4 on v3

--- a/solution.py
+++ b/solution.py
@@ -192,7 +192,7 @@
             jax.ShapeDtypeStruct((heads, width, tok), jnp.bfloat16),
             jax.ShapeDtypeStruct((seq, width), jnp.bfloat16),
         ],
-        compiler_params=pltpu.CompilerParams(vmem_limit_bytes=48 * 1024 * 1024),
+        compiler_params=pltpu.CompilerParams(vmem_limit_bytes=56 * 1024 * 1024),
         cost_estimate=pl.CostEstimate(
             flops=14 * tok * heads * seq * lat // 2, bytes_accessed=12 << 20, transcendentals=0
         ),
@@ -227,7 +227,8 @@
 
 
 def gather_kernel(
-    n_ctx, lat_ref, q_hbm, g_hbm, out_ref, q_out, g_out, own, q_in, g_in, g_wide,
+    n_ctx, lat_ref, q_hbm, g_hbm, out_ref, q_hbm_out, g_hbm_out, own, q_in, g_in, q_out,
+    g_out, g_wide,
     sems, pair_sems, local_sems,
 ):
     me, core, chip, sibling, chips = places(n_ctx)
@@ -260,6 +261,11 @@
         return carry
 
     lax.fori_loop(0, heads // 2, pack_heads, 0)
+    stores = [
+        pltpu.make_async_copy(q_out, q_hbm_out, local_sems.at[3]),
+        pltpu.make_async_copy(g_out, g_hbm_out, local_sems.at[4]),
+    ]
+    stores[0].start()
     loads[1].wait()
     for p in range(2):
         for lanes in range(g_wide.shape[0]):
@@ -270,6 +276,7 @@
                     lanes, pl.ds(head, half, stride=heads), :
                 ].astype(g_out.dtype)
 
+    stores[1].start()
     for k in range(1, chips):
         sends[k - 1].wait_recv()
         owner = lax.rem(chip + chips - k, chips) * 2 + core
@@ -280,6 +287,8 @@
         copy.wait_send()
     for copy in pairs:
         copy.wait()
+    for copy in stores:
+        copy.wait()
     keep.wait()
 
 
@@ -293,7 +302,7 @@
     out, q_cols, g_rows = pl.pallas_call(
         functools.partial(gather_kernel, n_ctx),
         in_specs=[vmem, hbm, hbm],
-        out_specs=[hbm, vmem, vmem],
+        out_specs=[hbm, hbm, hbm],
         out_shape=[
             jax.ShapeDtypeStruct((n_ctx, tok, width), kind),
             jax.ShapeDtypeStruct((2, width, total), kind),
@@ -303,20 +312,22 @@
             pltpu.VMEM((tok, width), kind),
             pltpu.VMEM((heads, width, tok), kind),
             pltpu.VMEM((tok * heads, lat), kind),
+            pltpu.VMEM((2, width, total), kind),
+            pltpu.VMEM((2, total, lat), kind),
             pltpu.VMEM((lat // LANES, total, LANES), jnp.float32),
             pltpu.SemaphoreType.DMA((2, n_ctx // 2)),
             pltpu.SemaphoreType.DMA((2, n_ctx // 2)),
-            pltpu.SemaphoreType.DMA((3,)),
+            pltpu.SemaphoreType.DMA((5,)),
         ],
         compiler_params=pltpu.CompilerParams(
-            collective_id=0, has_side_effects=True, vmem_limit_bytes=32 * 1024 * 1024
+            collective_id=0, has_side_effects=True, vmem_limit_bytes=56 * 1024 * 1024
         ),
     )(latents.T, jnp.transpose(queries, (1, 2, 0)), grad_out.reshape(tok * heads, lat))
     return out.reshape(n_ctx * tok, width), q_cols, g_rows
 
 
 def reduce_kernel(
-    n_ctx, n_head, part_ref, out_ref, pair_in, chip_out, chip_in, head_out, head_in, whole,
+    n_ctx, n_head, part_ref, out_ref, pair_in, chip_out, chip_in, head_out, head_in, whole, sum_own,
     pair_sems, chip_sems, head_sems, last_sems,
 ):
     me, core, chip, sibling, chips = places(n_ctx)
@@ -327,53 +338,74 @@
         [(sibling, z)] + [(other, z) for other in others] + [(me, other) for other in heads]
     )
     order = [lax.rem(chip + k, chips) for k in range(1, chips + 1)]
+    parts = part_ref.shape[1]
+    rows = part_ref.shape[2] // n_head
     pairs = [
-        transfer(
-            part_ref.at[target * 2 + 1 - core], pair_in.at[k], pair_sems, k, (sibling, z)
-        )
-        for k, target in enumerate(order)
+        [
+            transfer(
+                part_ref.at[target * 2 + 1 - core, s], pair_in.at[s, k], pair_sems.at[s], k,
+                (sibling, z),
+            )
+            for k, target in enumerate(order)
+        ]
+        for s in range(parts)
     ]
-    sends = []
-    total = None
-    for k, target in enumerate(order):
-        pairs[k].wait_recv()
-        total = part_ref[target * 2 + core].astype(jnp.float32) + pair_in[k].astype(jnp.float32)
-        if k < chips - 1:
-            chip_out[k] = total.astype(jnp.bfloat16)
-            sends.append(
-                transfer(chip_out.at[k], chip_in.at[k], chip_sems, k, (others[k], z))
+    sends, steps, lasts, totals = [], [], [], []
+    for s in range(parts):
+        sent = []
+        for k, target in enumerate(order):
+            pairs[s][k].wait_recv()
+            total = part_ref[target * 2 + core, s].astype(jnp.float32) + pair_in[s, k].astype(
+                jnp.float32
             )
-    for k, copy in enumerate(sends):
-        copy.wait_recv()
-        total = total + chip_in[k].astype(jnp.float32)
-    rows = total.shape[0] // n_head
-    for k in range(n_head):
-        head_out[k] = total[k * rows : (k + 1) * rows].astype(jnp.bfloat16)
-    steps = [
-        transfer(head_out.at[other], head_in.at[k], head_sems, k, (me, other))
-        for k, other in enumerate(heads)
-    ]
-    piece = head_out[z].astype(jnp.float32)
-    for k, copy in enumerate(steps):
-        copy.wait_recv()
-        piece = piece + head_in[k].astype(jnp.float32)
-    whole[z] = piece.astype(jnp.bfloat16)
-    lasts = [
-        transfer(whole.at[z], whole.at[z], last_sems, k, (me, other))
-        for k, other in enumerate(heads)
-    ]
-    for copy in lasts:
-        copy.wait_recv()
-    result = jnp.concatenate([whole[k] for k in range(n_head)], axis=0)
+            if k < chips - 1:
+                chip_out[s, k] = total.astype(jnp.bfloat16)
+                sent.append(
+                    transfer(
+                        chip_out.at[s, k], chip_in.at[s, k], chip_sems.at[s], k, (others[k], z)
+                    )
+                )
+        sum_own[s] = total
+        sends.append(sent)
+    for s in range(parts):
+        total = sum_own[s]
+        for k, copy in enumerate(sends[s]):
+            copy.wait_recv()
+            total = total + chip_in[s, k].astype(jnp.float32)
+        for k in range(n_head):
+            head_out[s, k] = total[k * rows : (k + 1) * rows].astype(jnp.bfloat16)
+        steps.append([
+            transfer(head_out.at[s, other], head_in.at[s, k], head_sems.at[s], k, (me, other))
+            for k, other in enumerate(heads)
+        ])
+    for s in range(parts):
+        piece = head_out[s, z].astype(jnp.float32)
+        for k, copy in enumerate(steps[s]):
+            copy.wait_recv()
+            piece = piece + head_in[s, k].astype(jnp.float32)
+        whole[s, z] = piece.astype(jnp.bfloat16)
+        lasts.append([
+            transfer(whole.at[s, z], whole.at[s, z], last_sems.at[s], k, (me, other))
+            for k, other in enumerate(heads)
+        ])
+    for copies in lasts:
+        for copy in copies:
+            copy.wait_recv()
+    result = jnp.concatenate(
+        [whole[s, k] for s in range(parts) for k in range(n_head)], axis=0
+    )
     out_ref[...] = result.astype(jnp.float32).T
-    for copy in pairs + sends + steps + lasts:
-        copy.wait_send()
+    for copies in pairs + sends + steps + lasts:
+        for copy in copies:
+            copy.wait_send()
 
 
 def reduce_parts(parts, n_ctx, n_head):
     seq, width = parts.shape
     tok = seq // n_ctx
-    rows = tok // n_head
+    splits = 2 if tok // (2 * n_head) >= 16 else 1
+    deep = tok // splits
+    rows = deep // n_head
     chips = n_ctx // 2
     kind = parts.dtype
     vmem = pl.BlockSpec(memory_space=pltpu.VMEM)
@@ -383,21 +415,22 @@
         out_specs=vmem,
         out_shape=jax.ShapeDtypeStruct((width, tok), jnp.float32),
         scratch_shapes=[
-            pltpu.VMEM((chips, tok, width), kind),
-            pltpu.VMEM((chips, tok, width), kind),
-            pltpu.VMEM((chips, tok, width), kind),
-            pltpu.VMEM((n_head, rows, width), kind),
-            pltpu.VMEM((n_head, rows, width), kind),
-            pltpu.VMEM((n_head, rows, width), kind),
-            pltpu.SemaphoreType.DMA((2, chips)),
-            pltpu.SemaphoreType.DMA((2, chips)),
-            pltpu.SemaphoreType.DMA((2, n_head)),
-            pltpu.SemaphoreType.DMA((2, n_head)),
+            pltpu.VMEM((splits, chips, deep, width), kind),
+            pltpu.VMEM((splits, chips, deep, width), kind),
+            pltpu.VMEM((splits, chips, deep, width), kind),
+            pltpu.VMEM((splits, n_head, rows, width), kind),
+            pltpu.VMEM((splits, n_head, rows, width), kind),
+            pltpu.VMEM((splits, n_head, rows, width), kind),
+            pltpu.VMEM((splits, deep, width), jnp.float32),
+            pltpu.SemaphoreType.DMA((splits, 2, chips)),
+            pltpu.SemaphoreType.DMA((splits, 2, chips)),
+            pltpu.SemaphoreType.DMA((splits, 2, n_head)),
+            pltpu.SemaphoreType.DMA((splits, 2, n_head)),
         ],
         compiler_params=pltpu.CompilerParams(
             collective_id=1, has_side_effects=True, vmem_limit_bytes=32 * 1024 * 1024
         ),
-    )(parts.reshape(n_ctx, tok, width))
+    )(parts.reshape(n_ctx, splits, deep, width))
     return out.T
 
 

time: 64.1 us -> 60.8 us (0.949)
  local copies, waits for them, and re-layouts: 6.28 us -> 2.03 us
    unnamed x13 -> x3, local copies, waits for them, and re-layouts: 6.28 us -> 2.03 us
    pallas_call x1, Pallas kernels: 13.7 us -> 14.8 us  [gather(): pl.pallas_call(functools.partial(gather_kernel, n_ctx), in_specs=[vmem, h...]
    pallas_call x1, Pallas kernels: 27 us -> 26.1 us  [reduce_parts(): pl.pallas_call(functools.partial(reduce_kernel, n_ctx, n_head), in_specs=...]
where the time goes in v4:
time: 60.8 us; the launch traced here: 60.5 us
  Pallas kernels  57.8 us (95%)
  local copies, waits for them, and re-layouts  2.03 us (3%)
  between operations  0.66 us (1%)
    pallas_call x1, Pallas kernels, reduce_parts(): pl.pallas_call(functools.partial(reduce_kernel, n_ctx, n_head), in_specs=...  26.1 us
    pallas_call x1, Pallas kernels, attention(): pl.pallas_call(functools.partial(attention_kernel, (n_ctx, half, heads, c...  17 us
    pallas_call x1, Pallas kernels, gather(): pl.pallas_call(functools.partial(gather_kernel, n_ctx), in_specs=[vmem, h...  14.8 us
    unnamed x3, local copies, waits for them, and re-layouts  2.03 us

profile of v4, /device:TPU:0, one launch (start us, length us, event | category | flops | bytes accessed | tf_op | source)
XLA Modules:
  0.0 60.5 jit_solution(5180126276601116206)
XLA Ops:
  0.6 14.8 %shard_map.76 = (bf16[8,128,576]{2,1,0:T(8,128)(2,1)}, bf16[2,576,1024]{2,1,0:T(8,128)(2,1)}, bf16[2,1024,512]{2,1,0:T(8,128)(2,1)}) custom-call(bf16[576,128]{1,0:T(8,128)(2,1)} %bitcast.12, bf16[16,576,128]{2,1,0:T(8,128)(2,1)} %bitcast.10, bf16[2048,512]{1,0:T(8,128)(2,1)} %bitcast.11), custom_call_target="tpu_custom_call" | custom-call | tf_op jit(solution)/shard_map/pallas_call | solution.py:302
  15.5 17.0 %shard_map.77 = (bf16[2048,512]{1,0:T(8,128)(2,1)}, bf16[16,576,128]{2,1,0:T(8,128)(2,1)}, bf16[1024,576]{1,0:T(8,128)(2,1)}) custom-call(s32[8]{0:T(128)} %order_ref.1, s32[1024]{0:T(1024)} %docs_ref.1, bf16[2,576,1024]{2,1,0:T(8,128)(2,1)} %get-tuple-element.9.q_ref, bf16[2,1024,512]{2,1,0:T(8,128)(2,1)} %get-tuple-element.10.g_ref, bf16[1024,576]{1,0:T(8,128)(2,1)} %bitcast.13), custom_call_target="tpu_custom_call" | custom-call | flops 7516192768 | bytes 12582912 | tf_op jit(solution)/shard_map/pallas_call | solution.py:163
  32.4 0.0 copy-start
  32.4 1.3 %copy-done = bf16[1024,576]{1,0:T(8,128)(2,1)S(1)} copy-done((bf16[1024,576]{1,0:T(8,128)(2,1)S(1)}, bf16[1024,576]{1,0:T(8,128)(2,1)}, u32[]{:S(2)}) %copy-start) | copy-done | bytes 1179672
  33.8 26.1 %shard_map.78 = f32[576,128]{1,0:T(8,128)S(1)} custom-call(bf16[8,2,64,576]{3,2,1,0:T(8,128)(2,1)S(1)} %bitcast.8), custom_call_target="tpu_custom_call" | custom-call | tf_op jit(solution)/shard_map/pallas_call | solution.py:412
  59.8 0.7 %copy.9 = f32[128,576]{0,1:T(8,128)} copy(f32[128,576]{0,1:T(8,128)S(1)} %bitcast.9) | data formatting | bytes 589824
Async XLA Ops:
  32.4 1.3 %copy-start = (bf16[1024,576]{1,0:T(8,128)(2,1)S(1)}, bf16[1024,576]{1,0:T(8,128)(2,1)}, u32[]{:S(2)}) copy-start(bf16[1024,576]{1,0:T(8,128)(2,1)} %get-tuple-element.14) | copy-start | bytes 3538948

commit v5 on v4

--- a/solution.py
+++ b/solution.py
@@ -11,7 +11,7 @@
 far_below = -1e30
 DOCS = 4
 KEY_TILE = 256
-COLS = 512
+COLS = 1024
 LANES = 128
 NT = (((1,), (1,)), ((), ()))
 NN = (((1,), (0,)), ((), ()))
@@ -105,23 +105,27 @@
         inverse = 1.0 / row_sum
         delta = weighted * inverse
         scaled = inverse * score_scale
-        out_acc[...] = jnp.zeros_like(out_acc)
-        q_acc[...] = jnp.zeros_like(q_acc)
-
-        def third_pass(i, carry):
+
+        def third_pass(i, first):
             at = tile_at(i)
             e = scores[i]
             probs = (e * inverse).astype(jnp.bfloat16)
             ds = (e * scaled * (grad_probs[i] - delta)).astype(jnp.bfloat16)
-            out_acc[...] += dot(probs, keys[at, :lat], TN)
-            q_acc[...] += dot(keys[at, :], ds, TN)
+            out_now = dot(probs, keys[at, :lat], TN)
+            q_now = dot(keys[at, :], ds, TN)
+            out_acc[...] = out_now if first else out_acc[...] + out_now
+            q_acc[...] = q_now if first else q_acc[...] + q_now
             key_term = dot(ds, q_ref[0, :, here], NT)
             value_term = dot(probs, g_ref[0, here, :], NN)
             grad_keys[at, :lat] += key_term[:, :lat] + value_term
             grad_keys[at, lat:] += key_term[:, lat:]
-            return carry
-
-        lax.fori_loop(0, tiles, third_pass, 0)
+
+        third_pass(0, True)
+
+        @pl.loop(1, tiles)
+        def _(i):
+            third_pass(i, False)
+
         for k in range(heads_now):
             head = chunk * heads_now + k
             mine = slice(k * half, (k + 1) * half)

time: 60.8 us -> 58.7 us (0.965)
  Pallas kernels: 57.8 us -> 55.4 us
    pallas_call x1, Pallas kernels: 26.1 us -> 22.3 us  [reduce_parts(): pl.pallas_call(functools.partial(reduce_kernel, n_ctx, n_head), in_specs=...]
    pallas_call x1, Pallas kernels: 17 us -> 18.2 us  [attention(): pl.pallas_call(functools.partial(attention_kernel, (n_ctx, half, heads, c...]
where the time goes in v5:
time: 58.7 us; the launch traced here: 58.1 us
  Pallas kernels  55.4 us (94%)
  local copies, waits for them, and re-layouts  2.03 us (3%)
  between operations  0.66 us (1%)
    pallas_call x1, Pallas kernels, reduce_parts(): pl.pallas_call(functools.partial(reduce_kernel, n_ctx, n_head), in_specs=...  22.3 us
    pallas_call x1, Pallas kernels, attention(): pl.pallas_call(functools.partial(attention_kernel, (n_ctx, half, heads, c...  18.2 us
    pallas_call x1, Pallas kernels, gather(): pl.pallas_call(functools.partial(gather_kernel, n_ctx), in_specs=[vmem, h...  14.8 us
    unnamed x3, local copies, waits for them, and re-layouts  2.03 us

profile of v5, /device:TPU:0, one launch (start us, length us, event | category | flops | bytes accessed | tf_op | source)
XLA Modules:
  0.0 58.1 jit_solution(10870935518602634984)
XLA Ops:
  0.6 14.8 %shard_map.76 = (bf16[8,128,576]{2,1,0:T(8,128)(2,1)}, bf16[2,576,1024]{2,1,0:T(8,128)(2,1)}, bf16[2,1024,512]{2,1,0:T(8,128)(2,1)}) custom-call(bf16[576,128]{1,0:T(8,128)(2,1)} %bitcast.12, bf16[16,576,128]{2,1,0:T(8,128)(2,1)} %bitcast.10, bf16[2048,512]{1,0:T(8,128)(2,1)} %bitcast.11), custom_call_target="tpu_custom_call" | custom-call | tf_op jit(solution)/shard_map/pallas_call | solution.py:306
  15.5 18.2 %shard_map.77 = (bf16[2048,512]{1,0:T(8,128)(2,1)}, bf16[16,576,128]{2,1,0:T(8,128)(2,1)}, bf16[1024,576]{1,0:T(8,128)(2,1)}) custom-call(s32[8]{0:T(128)} %order_ref.1, s32[1024]{0:T(1024)} %docs_ref.1, bf16[2,576,1024]{2,1,0:T(8,128)(2,1)} %get-tuple-element.9.q_ref, bf16[2,1024,512]{2,1,0:T(8,128)(2,1)} %get-tuple-element.10.g_ref, bf16[1024,576]{1,0:T(8,128)(2,1)} %bitcast.13), custom_call_target="tpu_custom_call" | custom-call | flops 7516192768 | bytes 12582912 | tf_op jit(solution)/shard_map/pallas_call | solution.py:167
  33.7 0.0 copy-start
  33.7 1.3 %copy-done = bf16[1024,576]{1,0:T(8,128)(2,1)S(1)} copy-done((bf16[1024,576]{1,0:T(8,128)(2,1)S(1)}, bf16[1024,576]{1,0:T(8,128)(2,1)}, u32[]{:S(2)}) %copy-start) | copy-done | bytes 1179672
  35.0 22.3 %shard_map.78 = f32[576,128]{1,0:T(8,128)S(1)} custom-call(bf16[8,2,64,576]{3,2,1,0:T(8,128)(2,1)S(1)} %bitcast.8), custom_call_target="tpu_custom_call" | custom-call | tf_op jit(solution)/shard_map/pallas_call | solution.py:416
  57.4 0.7 %copy.9 = f32[128,576]{0,1:T(8,128)} copy(f32[128,576]{0,1:T(8,128)S(1)} %bitcast.9) | data formatting | bytes 589824
Async XLA Ops:
  33.7 1.3 %copy-start = (bf16[1024,576]{1,0:T(8,128)(2,1)S(1)}, bf16[1024,576]{1,0:T(8,128)(2,1)}, u32[]{:S(2)}) copy-start(bf16[1024,576]{1,0:T(8,128)(2,1)} %get-tuple-element.14) | copy-start | bytes 3538948

commit v6 on v5

--- a/solution.py
+++ b/solution.py
@@ -332,16 +332,23 @@
 
 def reduce_kernel(
     n_ctx, n_head, part_ref, out_ref, pair_in, chip_out, chip_in, head_out, head_in, whole, sum_own,
+    mine, load_sems,
     pair_sems, chip_sems, head_sems, last_sems,
 ):
     me, core, chip, sibling, chips = places(n_ctx)
     z = lax.axis_index("head")
     others = [lax.rem(chip + k, chips) * 2 + core for k in range(1, chips)]
     heads = [lax.rem(z + k, n_head) for k in range(1, n_head)]
+    order = [lax.rem(chip + k, chips) for k in range(1, chips + 1)]
+    loads = [
+        pltpu.make_async_copy(part_ref.at[target * 2 + core], mine.at[k], load_sems.at[k])
+        for k, target in enumerate(order)
+    ]
+    for load in loads:
+        load.start()
     greet(
         [(sibling, z)] + [(other, z) for other in others] + [(me, other) for other in heads]
     )
-    order = [lax.rem(chip + k, chips) for k in range(1, chips + 1)]
     parts = part_ref.shape[1]
     rows = part_ref.shape[2] // n_head
     pairs = [
@@ -354,14 +361,14 @@
         ]
         for s in range(parts)
     ]
-    sends, steps, lasts, totals = [], [], [], []
+    for load in loads:
+        load.wait()
+    sends, steps, lasts = [], [], []
     for s in range(parts):
         sent = []
         for k, target in enumerate(order):
             pairs[s][k].wait_recv()
-            total = part_ref[target * 2 + core, s].astype(jnp.float32) + pair_in[s, k].astype(
-                jnp.float32
-            )
+            total = mine[k, s].astype(jnp.float32) + pair_in[s, k].astype(jnp.float32)
             if k < chips - 1:
                 chip_out[s, k] = total.astype(jnp.bfloat16)
                 sent.append(
@@ -415,7 +422,7 @@
     vmem = pl.BlockSpec(memory_space=pltpu.VMEM)
     out = pl.pallas_call(
         functools.partial(reduce_kernel, n_ctx, n_head),
-        in_specs=[vmem],
+        in_specs=[pl.BlockSpec(memory_space=pl.ANY)],
         out_specs=vmem,
         out_shape=jax.ShapeDtypeStruct((width, tok), jnp.float32),
         scratch_shapes=[
@@ -426,13 +433,15 @@
             pltpu.VMEM((splits, n_head, rows, width), kind),
             pltpu.VMEM((splits, n_head, rows, width), kind),
             pltpu.VMEM((splits, deep, width), jnp.float32),
+            pltpu.VMEM((chips, splits, deep, width), kind),
+            pltpu.SemaphoreType.DMA((chips,)),
             pltpu.SemaphoreType.DMA((splits, 2, chips)),
             pltpu.SemaphoreType.DMA((splits, 2, chips)),
             pltpu.SemaphoreType.DMA((splits, 2, n_head)),
             pltpu.SemaphoreType.DMA((splits, 2, n_head)),
         ],
         compiler_params=pltpu.CompilerParams(
-            collective_id=1, has_side_effects=True, vmem_limit_bytes=32 * 1024 * 1024
+            collective_id=1, has_side_effects=True, vmem_limit_bytes=56 * 1024 * 1024
         ),
     )(parts.reshape(n_ctx, splits, deep, width))
     return out.T

time: 58.7 us -> 59.5 us (1.014); the launches traced: 58.1 us -> 59.8 us
  Pallas kernels: 55.4 us -> 57.5 us
    pallas_call x1, Pallas kernels: 22.3 us -> 27 us  [reduce_parts(): pl.pallas_call(functools.partial(reduce_kernel, n_ctx, n_head), in_specs=...]
    pallas_call x1, Pallas kernels: 18.2 us -> 15.7 us  [attention(): pl.pallas_call(functools.partial(attention_kernel, (n_ctx, half, heads, c...]
    unnamed x3 -> x1, local copies, waits for them, and re-layouts: 2.03 us -> 1.69 us
where the time goes in v6:
time: 59.5 us; the launch traced here: 59.8 us
  Pallas kernels  57.5 us (97%)
  local copies, waits for them, and re-layouts  1.69 us (3%)
  between operations  0.65 us (1%)
    pallas_call x1, Pallas kernels, reduce_parts(): pl.pallas_call(functools.partial(reduce_kernel, n_ctx, n_head), in_specs=...  27 us
    pallas_call x1, Pallas kernels, attention(): pl.pallas_call(functools.partial(attention_kernel, (n_ctx, half, heads, c...  15.7 us
    pallas_call x1, Pallas kernels, gather(): pl.pallas_call(functools.partial(gather_kernel, n_ctx), in_specs=[vmem, h...  14.8 us
    unnamed x1, local copies, waits for them, and re-layouts  1.69 us

profile of v6, /device:TPU:0, one launch (start us, length us, event | category | flops | bytes accessed | tf_op | source)
XLA Modules:
  0.0 59.8 jit_solution(17526474986177734091)
XLA Ops:
  0.6 14.8 %shard_map.76 = (bf16[8,128,576]{2,1,0:T(8,128)(2,1)}, bf16[2,576,1024]{2,1,0:T(8,128)(2,1)}, bf16[2,1024,512]{2,1,0:T(8,128)(2,1)}) custom-call(bf16[576,128]{1,0:T(8,128)(2,1)} %bitcast.12, bf16[16,576,128]{2,1,0:T(8,128)(2,1)} %bitcast.8, bf16[2048,512]{1,0:T(8,128)(2,1)} %bitcast.9), custom_call_target="tpu_custom_call" | custom-call | tf_op jit(solution)/shard_map/pallas_call | solution.py:306
  15.5 15.7 %shard_map.77 = (bf16[2048,512]{1,0:T(8,128)(2,1)}, bf16[16,576,128]{2,1,0:T(8,128)(2,1)}, bf16[1024,576]{1,0:T(8,128)(2,1)}) custom-call(s32[8]{0:T(128)} %order_ref.1, s32[1024]{0:T(1024)} %docs_ref.1, bf16[2,576,1024]{2,1,0:T(8,128)(2,1)} %get-tuple-element.9.q_ref, bf16[2,1024,512]{2,1,0:T(8,128)(2,1)} %get-tuple-element.10.g_ref, bf16[1024,576]{1,0:T(8,128)(2,1)} %bitcast.13), custom_call_target="tpu_custom_call" | custom-call | flops 7516192768 | bytes 12582912 | tf_op jit(solution)/shard_map/pallas_call | solution.py:167
  31.2 27.0 %shard_map.78 = f32[576,128]{1,0:T(8,128)} custom-call(bf16[8,2,64,576]{3,2,1,0:T(8,128)(2,1)} %bitcast.10), custom_call_target="tpu_custom_call" | custom-call | tf_op jit(solution)/shard_map/pallas_call | solution.py:423
  58.1 1.7 %copy.9 = f32[128,576]{0,1:T(8,128)} copy(f32[128,576]{0,1:T(8,128)} %bitcast.11) | data formatting | bytes 589824
